TPU v7x, 128 devices: a whole 4x4x4 slice. The times are simulated.
128 devices in a mesh: member: 4 (over z_lo, core), slab: 32 (over x, z_hi, y).
Axes of the slice: x: 4, y: 4, z: 4 (z_hi: 2, z_lo: 2; z = z_hi * 2 + z_lo), core: 2. Of those that a mesh axis runs over, the one named last changes fastest.
Arguments:
- structure: float32 [8, 256, 256, 256], P('member', 'slab'), may hold values from 0.02 to 0.98
- upstream: float32 [8, 256, 256, 256], P('member', 'slab'), may hold values from -6 to 6
- noise: float32 [2, 8, 256, 256, 256], P(None, 'member', None, 'slab'), may hold values from -6 to 6
- density: float32 [256, 256, 256], P('member', 'slab'), may hold values from 0.1 to 10
Outputs:
- density_grad: float32 [256, 256, 256], P('member', 'slab')
All inputs are finite; a program needn't handle non-finite values.
Results may differ from a plain program's by a relative error of at most 0.0001.
Values sent between devices are 32-bit elements; how exact they have to be, the bound alone decides.
No kernel may reach another device: no remote copies, remote signals or barrier semaphores. Data moves between devices by JAX's collectives and lax.ppermute only.
A program may use at most 128 MiB of HBM per device.

v0:
```python
import math

import jax
import jax.numpy as jnp
from jax import lax
from jax.sharding import PartitionSpec as P

sigmoid_slope = 8.0


def dft_tables(length_grid):
    indices = jnp.arange(length_grid, dtype=jnp.int32)
    products = indices[:, None] * indices[None, :] % length_grid
    angles = products.astype(jnp.float32) * (2.0 * math.pi / length_grid)
    factor_norm = 1.0 / math.sqrt(length_grid)
    return (jnp.cos(angles) * factor_norm, jnp.sin(angles) * factor_norm)


def contract(form, values, table):
    return jnp.einsum(
        form, values, table, precision=lax.Precision.HIGHEST, preferred_element_type=jnp.float32
    )


def body(structure, upstream, noise, density):
    length_grid = structure.shape[-1]
    cosine_table, sine_table = dft_tables(length_grid)
    field_grad = upstream * sigmoid_slope * structure * (1.0 - structure)
    after_z_real = contract("mxyz,zk->mxyk", field_grad, cosine_table)
    after_z_imag = -contract("mxyz,zk->mxyk", field_grad, sine_table)
    after_y_real = contract("mxyz,yk->mxkz", after_z_real, cosine_table) + contract(
        "mxyz,yk->mxkz", after_z_imag, sine_table
    )
    after_y_imag = contract("mxyz,yk->mxkz", after_z_imag, cosine_table) - contract(
        "mxyz,yk->mxkz", after_z_real, sine_table
    )
    planes = jnp.stack((after_y_real, after_y_imag))
    slab_block = lax.all_to_all(planes, "slab", split_axis=3, concat_axis=2, tiled=True)
    real_part = slab_block[0]
    imag_part = slab_block[1]
    out_real = contract("mxyz,xk->mkyz", real_part, cosine_table) + contract(
        "mxyz,xk->mkyz", imag_part, sine_table
    )
    out_imag = contract("mxyz,xk->mkyz", imag_part, cosine_table) - contract(
        "mxyz,xk->mkyz", real_part, sine_table
    )
    spectrum = jnp.stack((out_real, out_imag))
    local_sum = jnp.sum(noise[0] * spectrum[0] + noise[1] * spectrum[1], axis=0)
    summed = lax.psum_scatter(local_sum, "member", scatter_dimension=0, tiled=True)
    return summed / (2.0 * jnp.sqrt(density))


def solution(mesh):
    in_specs = (
        P("member", "slab", None, None),
        P("member", "slab", None, None),
        P(None, "member", None, "slab", None),
        P("member", "slab", None),
    )
    out_specs = P("member", "slab", None)
    return jax.shard_map(body, mesh=mesh, in_specs=in_specs, out_specs=out_specs, check_vma=False)
```

profile of v0, /device:TPU:1, one launch (start us, length us, event | category | flops | bytes accessed | tf_op | source)
XLA Modules:
  0.0 292.6 jit_solution(4273190068395315563)
XLA Ops:
  6.5 0.0 copy-start.1
  6.5 0.0 copy-start
  6.5 8.4 %fusion.16 = f32[2,8,256,256]{3,2,1,0:T(8,128)S(1)} fusion(f32[2,8,256,256]{3,2,1,0:T(8,128)} %param.4, f32[2,8,256,256]{3,2,1,0:T(8,128)} %param.5), kind=kOutput, calls=%fused_computation.21 | convolution fusion | flops 3226402816 | bytes 12582912 | tf_op jit(solution)/shard_map/mxyz,zk->mxyk/dot_general | solution.py:20
  14.9 0.0 copy-done.1
  14.9 0.0 copy-done
  14.9 4.6 %fusion.17 = f32[2,8,256,256]{3,2,1,0:T(8,128)S(1)} fusion(f32[2,8,256,256]{3,2,1,0:T(8,128)S(1)} %copy-done, f32[2,8,256,256]{3,2,1,0:T(8,128)S(1)} %copy-done.1), kind=kOutput, calls=%fused_computation.22 | convolution fusion | flops 3226402816 | bytes 12582912 | tf_op jit(solution)/shard_map/mxyz,zk->mxyk/dot_general | solution.py:20
  19.5 4.8 %fusion.26 = f32[256,2,8,256]{3,0,2,1:T(8,128)S(1)} fusion(f32[2,8,256,256]{3,2,1,0:T(8,128)S(1)} %fusion.17), kind=kOutput, calls=%fused_computation.35 | convolution fusion | flops 3222208512 | bytes 8388608 | tf_op jit(solution)/shard_map/mxyz,yk->mxkz/dot_general | solution.py:20
  24.3 5.2 %fusion.33 = f32[256,2,8,256]{3,0,2,1:T(8,128)S(1)} fusion(f32[2,8,256,256]{3,2,1,0:T(8,128)S(1)} %fusion.17), kind=kOutput, calls=%fused_computation.42 | convolution fusion | flops 3222208512 | bytes 8388608 | tf_op jit(solution)/shard_map/mxyz,yk->mxkz/dot_general | solution.py:20
  29.5 5.2 %add_bitcast_fusion = f32[1,2,8,256,256]{4,3,2,1,0:T(8,128)S(1)} fusion(f32[256,2,8,256]{3,0,2,1:T(8,128)S(1)} %fusion.33, f32[2,8,256,256]{3,2,1,0:T(8,128)S(1)} %fusion.16), kind=kOutput, calls=%fused_computation.11 | convolution fusion | flops 3224305664 | bytes 12582912 | tf_op jit(solution)/shard_map/mxyz,yk->mxkz/dot_general | solution.py:20
  34.7 5.3 %subtract_bitcast_fusion = f32[1,2,8,256,256]{4,3,2,1,0:T(8,128)S(1)} fusion(f32[256,2,8,256]{3,0,2,1:T(8,128)S(1)} %fusion.26, f32[2,8,256,256]{3,2,1,0:T(8,128)S(1)} %fusion.16), kind=kOutput, calls=%fused_computation.10 | convolution fusion | flops 3224305664 | bytes 12582912 | tf_op jit(solution)/shard_map/mxyz,yk->mxkz/dot_general | solution.py:20
  40.0 0.9 pad_maximum_fusion
  40.9 8.1 %copy.14 = f32[2,2,8,256,256]{4,2,1,0,3:T(8,128)} copy(f32[2,2,8,256,256]{4,3,2,1,0:T(8,128)S(1)} %pad_maximum_fusion) | data formatting | bytes 16777216 | tf_op jit(solution)/shard_map/stack | solution.py:37
  49.0 11.3 %all-to-all-start = ((f32[2,2,8,256,256]{4,2,1,0,3:T(8,128)}), f32[2,2,8,256,256]{4,2,1,0,3:T(8,128)}, u32[]{:S(2)}, u32[]{:S(2)}) async-start(f32[2,2,8,256,256]{4,2,1,0,3:T(8,128)} %copy.14), calls=%async_computation | async-start | bytes 16777216 | tf_op jit(solution)/shard_map/all_to_all | solution.py:38
  60.3 0.0 reduce-scatter.2.cloned.1.call-start
  60.3 7.2 %fusion.112 = (f32[1,2,256,8,256]{4,3,2,1,0:T(8,128)}, f32[1,2,256,8,256]{4,3,2,1,0:T(8,128)}) fusion(f32[2,2,256,8,256]{4,3,2,1,0:T(8,128)} %param.6), kind=kLoop, calls=%fused_computation.113 | loop fusion | bytes 16777216 | tf_op jit(solution)/shard_map/slice | solution.py:48
  67.6 146.2 %all-to-all-done = f32[2,2,8,256,256]{4,2,1,0,3:T(8,128)} async-done(((f32[2,2,8,256,256]{4,2,1,0,3:T(8,128)}), f32[2,2,8,256,256]{4,2,1,0,3:T(8,128)}, u32[]{:S(2)}, u32[]{:S(2)}) %all-to-all-start) | async-done | bytes 8388640 | tf_op jit(solution)/shard_map/all_to_all | solution.py:38
  213.7 4.3 %copy.45 = f32[2,2,8,32,8,256]{5,2,3,4,1,0:T(8,128)S(1)} copy(f32[2,2,8,32,8,256]{5,2,1,0,4,3:T(8,128)} %bitcast.13) | data formatting | bytes 16777216 | tf_op jit(solution)/shard_map/all_to_all | solution.py:38
  218.0 5.2 %fusion.6 = f32[256,2,8,256]{3,0,2,1:T(8,128)S(1)} fusion(f32[2,2,32,8,8,256]{5,3,2,4,1,0:T(8,128)S(1)} %bitcast.70), kind=kOutput, calls=%fused_computation.15 | convolution fusion | flops 3222208512 | bytes 8388608 | tf_op jit(solution)/shard_map/mxyz,xk->mkyz/dot_general | solution.py:20
  223.3 5.2 %fusion.4 = f32[256,2,8,256]{3,0,2,1:T(8,128)S(1)} fusion(f32[2,2,32,8,8,256]{5,3,2,4,1,0:T(8,128)S(1)} %bitcast.71), kind=kOutput, calls=%fused_computation.13 | convolution fusion | flops 3222208512 | bytes 8388608 | tf_op jit(solution)/shard_map/mxyz,xk->mkyz/dot_general | solution.py:20
  228.5 5.4 %fusion.5 = f32[256,2,8,256]{3,0,2,1:T(8,128)S(1)} fusion(f32[2,2,32,8,8,256]{5,3,2,4,1,0:T(8,128)S(1)} %bitcast.72), kind=kOutput, calls=%fused_computation.14 | convolution fusion | flops 3222208512 | bytes 8388608 | tf_op jit(solution)/shard_map/mxyz,xk->mkyz/dot_general | solution.py:20
  233.9 0.0 copy-start.2
  233.9 13.8 %fusion.2 = f32[256,8,256]{2,0,1:T(8,128)} fusion(f32[1,2,256,8,256]{4,3,2,1,0:T(8,128)} %get-tuple-element.6, f32[1,2,256,8,256]{4,3,2,1,0:T(8,128)} %get-tuple-element.5, f32[256,2,8,256]{3,0,2,1:T(8,128)S(1)} %fusion.6, f32[256,2,8,256]{3,0,2,1:T(8,128)S(1)} %fusion.4, f32[256,2,8,256]{3,0,2,1:T(8,128)S(1)} %fusion.5, ...), kind=kOutput, calls=%fused_computation.7 | convolution fusion | flops 3227975680 | bytes 27262976 | tf_op jit(solution)/shard_map/mxyz,xk->mkyz/dot_general | solution.py:20
  247.7 0.0 reduce-scatter.2.cloned.1.call-update
  247.8 35.4 %reduce-scatter.2.cloned.1.call-done = f32[64,8,256]{2,0,1:T(8,128)} async-done(((f32[256,8,256]{2,0,1:T(8,128)}), f32[64,8,256]{2,0,1:T(8,128)}) %reduce-scatter.2.cloned.1.call-update) | async-done | bytes 524304 | tf_op jit(solution)/shard_map/reduce_scatter | solution.py:49
  283.1 0.0 copy-done.2
  283.1 1.3 fusion.19
  284.4 1.1 copy.18
Async XLA Ops:
  6.5 8.4 %copy-start.1 = (f32[2,8,256,256]{3,2,1,0:T(8,128)S(1)}, f32[2,8,256,256]{3,2,1,0:T(8,128)}, u32[]{:S(2)}) copy-start(f32[2,8,256,256]{3,2,1,0:T(8,128)} %param.5) | copy-start | bytes 12582916
  6.5 8.4 %copy-start = (f32[2,8,256,256]{3,2,1,0:T(8,128)S(1)}, f32[2,8,256,256]{3,2,1,0:T(8,128)}, u32[]{:S(2)}) copy-start(f32[2,8,256,256]{3,2,1,0:T(8,128)} %param.4) | copy-start | bytes 12582916
  49.0 164.7 %all-to-all-start = ((f32[2,2,8,256,256]{4,2,1,0,3:T(8,128)}), f32[2,2,8,256,256]{4,2,1,0,3:T(8,128)}, u32[]{:S(2)}, u32[]{:S(2)}) async-start(f32[2,2,8,256,256]{4,2,1,0,3:T(8,128)} %copy.14), calls=%async_computation | async-start | bytes 16777216 | tf_op jit(solution)/shard_map/all_to_all | solution.py:38
  60.3 222.8 %reduce-scatter.2.cloned.1.call-start = ((), (), s32[]{:S(2)}) async-start(), calls=%async_computation.2 | async-start | bytes 2621440 | tf_op jit(solution)/shard_map/reduce_scatter | solution.py:49
  233.9 49.2 %copy-start.2 = (f32[64,8,256]{2,1,0:T(8,128)S(1)}, f32[64,8,256]{2,1,0:T(8,128)}, u32[]{:S(2)}) copy-start(f32[64,8,256]{2,1,0:T(8,128)} %param.7) | copy-start | bytes 1572868
Sparse Core Ops, SparseCore 0:
  247.9 35.1 reduce-scatter.1
where the time goes:
time: 296 us; the launch traced here: 293 us
  waiting for transfers between devices  182 us (61%)
  matrix products  63.1 us (21%)
  local copies, waits for them, and re-layouts  20.7 us (7%)
  between operations  13.7 us (5%)
  starting transfers between devices  11.3 us (4%)
    all_to_all x1, waiting for transfers between devices, body(): lax.all_to_all(planes, 'slab', split_axis=3, concat_axis=2, tiled=True)  146 us
    dot_general x10, matrix products, contract(): jnp.einsum(form, values, table, precision=lax.Precision.HIGHEST, preferre...  63.1 us
    reduce_scatter x1, waiting for transfers between devices, body(): lax.psum_scatter(local_sum, 'member', scatter_dimension=0, tiled=True)  35.4 us
    all_to_all x1, starting transfers between devices, body(): lax.all_to_all(planes, 'slab', split_axis=3, concat_axis=2, tiled=True)  11.3 us
    another operation x1, local copies, waits for them, and re-layouts, body(): planes = jnp.stack((after_y_real, after_y_imag))  8.08 us
    slice x1, local copies, waits for them, and re-layouts, body(): local_sum = jnp.sum(noise[0] * spectrum[0] + noise[1] * spectrum[1], axis=0)  7.23 us
  transfers between devices with their start and end apart: 2, of which 2 were waited for; matrix products, arithmetic and copies ran while one was open for 2% of the time, Pallas kernels for 0%

commit v1 on v0

v1 whole, which is shorter than its diff:
```python
import math

import jax
import jax.numpy as jnp
import ml_dtypes
import numpy as np
from jax import lax
from jax.experimental import pallas as pl
from jax.experimental.pallas import tpu as pltpu
from jax.sharding import PartitionSpec as P

sigmoid_slope = 8.0
grid_length = 256
half = grid_length // 2
devices_slab = 32
devices_member = 4


def waves(rows, columns):
    angles = (np.outer(rows, columns) % grid_length) * (2.0 * math.pi / grid_length)
    return np.cos(angles) / 16.0, -np.sin(angles) / 16.0


def split_table(table):
    high = table.astype(np.float32).astype(ml_dtypes.bfloat16)
    low = (table - high.astype(np.float64)).astype(np.float32).astype(ml_dtypes.bfloat16)
    return high, low


def along_z_table():
    real, imag = waves(np.arange(grid_length), np.arange(grid_length))
    high, low = split_table(np.concatenate((real, imag), axis=1))
    return np.concatenate((high, high, low), axis=0)


def halves_table(order):
    tables = []
    for parity in range(2):
        real, imag = waves(order, np.arange(parity, grid_length, 2))
        full = np.concatenate(
            (np.concatenate((real, -imag), axis=1), np.concatenate((imag, real), axis=1)), axis=0
        )
        high, low = split_table(full)
        tables.append(np.concatenate((high, low, high), axis=1))
    return np.stack(tables)


def split_rows(values):
    high = values.astype(jnp.bfloat16)
    low = (values - high.astype(jnp.float32)).astype(jnp.bfloat16)
    return jnp.concatenate((high, high, low), axis=0)


def dot(left, right):
    return jnp.dot(left, right, preferred_element_type=jnp.float32)


def planes_kernel(left_ref, right_ref, left_up_ref, right_up_ref, z_ref, y_ref, out_ref):
    def field_grad(parity, structure_ref, upstream_ref):
        rows = pl.ds(parity, half, stride=2)
        structure = structure_ref[0, 0, rows, :]
        return upstream_ref[0, 0, rows, :] * sigmoid_slope * structure * (1.0 - structure)

    field = jnp.concatenate(
        [
            jnp.concatenate(
                (
                    field_grad(parity, left_ref, left_up_ref),
                    field_grad(parity, right_ref, right_up_ref),
                ),
                axis=1,
            )
            for parity in range(2)
        ],
        axis=0,
    )
    high = field.astype(jnp.bfloat16)
    low = (field - high.astype(jnp.float32)).astype(jnp.bfloat16)
    after_z = dot(jnp.concatenate((high, low, high), axis=1), z_ref[...])
    sums = []
    for parity in range(2):
        rows = after_z[parity * half : (parity + 1) * half]
        stacked = jnp.concatenate((rows[:, :grid_length], rows[:, grid_length:]), axis=0)
        sums.append(dot(y_ref[parity], split_rows(stacked)))
    below, above = sums[0] + sums[1], sums[0] - sums[1]
    for part in range(2):
        rows = slice(part * half, (part + 1) * half)
        out_ref[:16, part, 0, 0] = below[rows].reshape(16, 8, grid_length)
        out_ref[16:, part, 0, 0] = above[rows].reshape(16, 8, grid_length)


def planes(structure, upstream):
    members, depth = structure.shape[:2]
    blocks = [
        pl.BlockSpec((1, 1, grid_length, 128), lambda m, x, side=side: (m, x, 0, side))
        for side in range(2)
    ]
    return pl.pallas_call(
        planes_kernel,
        out_shape=jax.ShapeDtypeStruct(
            (devices_slab, 2, members, depth, 8, grid_length), jnp.float32
        ),
        grid=(members, depth),
        in_specs=[
            *blocks,
            *blocks,
            pl.BlockSpec((768, 512), lambda m, x: (0, 0)),
            pl.BlockSpec((2, 256, 768), lambda m, x: (0, 0, 0)),
        ],
        out_specs=pl.BlockSpec(
            (devices_slab, 2, 1, 1, 8, grid_length), lambda m, x: (0, 0, m, x, 0, 0)
        ),
        compiler_params=pltpu.CompilerParams(vmem_limit_bytes=32 * 1024 * 1024),
        name="planes",
    )(structure, structure, upstream, upstream, along_z_table(), halves_table(np.arange(half)))


def sums_kernel(place_ref, real_ref, imag_ref, noise_ref, x_ref, out_ref):
    first = pl.program_id(1) == 0
    z_lo, core = place_ref[0], place_ref[1]
    real_ref = real_ref.reshape(2048, 128)
    imag_ref = imag_ref.reshape(2048, 128)
    for pair in range(4):
        spectra = []
        for parity in range(2):
            stacked = jnp.concatenate(
                [
                    jnp.concatenate(
                        [
                            ref[pl.ds(parity * 8 + 2 * pair + side, half, stride=16), :]
                            for side in range(2)
                        ],
                        axis=1,
                    )
                    for ref in (real_ref, imag_ref)
                ],
                axis=0,
            )
            spectra.append(dot(x_ref[parity], split_rows(stacked)))
        for z, spectrum in enumerate((spectra[0] + spectra[1], spectra[0] - spectra[1])):
            for h in range(2):
                block = jnp.bitwise_xor(z_lo, z) * 2 + jnp.bitwise_xor(core, 1 - h)
                for side in range(2):
                    k = 2 * pair + side
                    lanes = slice(side * 128, (side + 1) * 128)
                    rows = pl.ds(k, 64, stride=8)
                    value = (
                        noise_ref[0, 0, block, rows, :] * spectrum[h * 64 : h * 64 + 64, lanes]
                        + noise_ref[1, 0, block, rows, :]
                        * spectrum[half + h * 64 : half + h * 64 + 64, lanes]
                    )
                    before = jnp.where(first, 0.0, out_ref[h, z, k])
                    out_ref[h, z, k] = before + value


def sums(received, noise, x_table, place):
    members = received.shape[2]
    parts = [
        pl.BlockSpec(
            (devices_slab, 1, 1, 64, 128), lambda z, m, p, part=part: (0, part, m, 0, z)
        )
        for part in range(2)
    ]
    return pl.pallas_call(
        sums_kernel,
        out_shape=jax.ShapeDtypeStruct((2, 2, 8, 64, grid_length), jnp.float32),
        grid_spec=pltpu.PrefetchScalarGridSpec(
            num_scalar_prefetch=1,
            grid=(2, members),
            in_specs=parts
            + [
                pl.BlockSpec((2, 1, 4, 512, 128), lambda z, m, p: (0, m, 0, 0, z)),
                pl.BlockSpec((2, 256, 768), lambda z, m, p: (0, 0, 0)),
            ],
            out_specs=pl.BlockSpec((2, 2, 8, 64, 128), lambda z, m, p: (0, 0, 0, 0, z)),
        ),
        compiler_params=pltpu.CompilerParams(vmem_limit_bytes=48 * 1024 * 1024),
        name="sums",
    )(
        place,
        received.reshape(devices_slab, 2, members, 64, grid_length),
        received.reshape(devices_slab, 2, members, 64, grid_length),
        noise.reshape(2, members, 4, 512, grid_length),
        x_table,
    )


def swap(values, flip):
    return lax.ppermute(values, "member", [(i, i ^ flip) for i in range(devices_member)])


def body(structure, upstream, noise, density):
    index = lax.axis_index("member")
    z_lo, core = index // 2, index % 2
    low, high = np.arange(64), np.arange(64, 128)
    x_tables = np.stack(
        [
            halves_table(np.concatenate(order)).astype(np.float32)
            for order in ((high, low), (low, high))
        ]
    ).astype(ml_dtypes.bfloat16)
    signs = jnp.stack((jnp.float32(1), 1.0 - 2.0 * z_lo.astype(jnp.float32)))
    x_table = jnp.where(core == 0, x_tables[0], x_tables[1]) * signs[:, None, None].astype(
        jnp.bfloat16
    )
    place = jnp.stack((z_lo, core)).astype(jnp.int32)
    sent = planes(structure, upstream)
    sent, x_table, place = lax.optimization_barrier((sent, x_table, place))
    received = lax.all_to_all(sent, "slab", split_axis=0, concat_axis=0, tiled=True)
    received, noise, density, x_table, place = lax.optimization_barrier(
        (received, noise, density, x_table, place)
    )
    partial = sums(received, noise, x_table, place)
    on_chip = partial[1] + swap(partial[0], 1)
    total = on_chip[0] + swap(on_chip[1], 2)
    return jnp.transpose(total, (1, 0, 2)) / (2.0 * jnp.sqrt(density))


def solution(mesh):
    in_specs = (
        P("member", "slab", None, None),
        P("member", "slab", None, None),
        P(None, "member", None, "slab", None),
        P("member", "slab", None),
    )
    out_specs = P("member", "slab", None)
    return jax.shard_map(body, mesh=mesh, in_specs=in_specs, out_specs=out_specs, check_vma=False)
```

time: 296 us -> 159 us (0.54)
  waiting for transfers between devices: 182 us -> 14.7 us
  blocking collectives: 0 us -> 106 us
  matrix products: 63.1 us -> 0 us
  Pallas kernels: 0 us -> 24.3 us
  between operations: 13.7 us -> 0.06 us
  local copies, waits for them, and re-layouts: 20.7 us -> 7.85 us
  starting transfers between devices: 11.3 us -> 3.63 us
    all_to_all x1 -> x0, waiting for transfers between devices: 146 us -> none  [body(): lax.all_to_all(planes, 'slab', split_axis=3, concat_axis=2, tiled=True)]
    all_to_all x0 -> x1, blocking collectives: none -> 106 us  [body(): lax.all_to_all(sent, 'slab', split_axis=0, concat_axis=0, tiled=True)]
    dot_general x10 -> x0, matrix products: 63.1 us -> none  [contract(): jnp.einsum(form, values, table, precision=lax.Precision.HIGHEST, preferre...]
    reduce_scatter x1 -> x0, waiting for transfers between devices: 35.4 us -> none  [body(): lax.psum_scatter(local_sum, 'member', scatter_dimension=0, tiled=True)]
    pallas_call x0 -> x2, Pallas kernels: none -> 24.3 us  [the longest x1 13.2 us: planes(): pl.pallas_call(planes_kernel, out_shape=jax.ShapeDtypeStruct((devices_sla...]
    ppermute x0 -> x2, waiting for transfers between devices: none -> 14.7 us  [swap(): lax.ppermute(values, 'member', [(i, i ^ flip) for i in range(devices_memb...]
    all_to_all x1 -> x0, starting transfers between devices: 11.3 us -> none  [body(): lax.all_to_all(planes, 'slab', split_axis=3, concat_axis=2, tiled=True)]
    another operation x1 -> x0, local copies, waits for them, and re-layouts: 8.08 us -> none  [body(): planes = jnp.stack((after_y_real, after_y_imag))]
  transfers between devices with their start and end apart: 2 -> 2, of which waited for: 2 -> 2; matrix products, arithmetic and copies ran while one was open for 2% -> 0% of each run, Pallas kernels for 0% -> 0%
where the time goes in v1:
time: 159 us; the launch traced here: 158 us
  blocking collectives  106 us (67%)
  Pallas kernels  24.3 us (15%)
  waiting for transfers between devices  14.7 us (9%)
  local copies, waits for them, and re-layouts  7.85 us (5%)
  starting transfers between devices  3.63 us (2%)
  other arithmetic  1.84 us (1%)
    all_to_all x1, blocking collectives, body(): lax.all_to_all(sent, 'slab', split_axis=0, concat_axis=0, tiled=True)  106 us
    ppermute x2, waiting for transfers between devices, swap(): lax.ppermute(values, 'member', [(i, i ^ flip) for i in range(devices_memb...  14.7 us
    pallas_call x1, Pallas kernels, planes(): pl.pallas_call(planes_kernel, out_shape=jax.ShapeDtypeStruct((devices_sla...  13.2 us
    pallas_call x1, Pallas kernels, sums(): pl.pallas_call(sums_kernel, out_shape=jax.ShapeDtypeStruct((2, 2, 8, 64,...  11.1 us
    unnamed x10, local copies, waits for them, and re-layouts  6.64 us
    ppermute x2, starting transfers between devices, swap(): lax.ppermute(values, 'member', [(i, i ^ flip) for i in range(devices_memb...  3.63 us
  transfers between devices with their start and end apart: 2, of which 2 were waited for; matrix products, arithmetic and copies ran while one was open for 0% of the time, Pallas kernels for 0%

profile of v1, /device:TPU:1, one launch (start us, length us, event | category | flops | bytes accessed | tf_op | source)
XLA Modules:
  0.0 158.3 jit_solution(4223800970380991678)
XLA Ops:
  0.0 0.1 pad_add_fusion.place_ref
  0.1 0.1 pad_maximum_fusion
  0.2 1.3 select_multiply_fusion.x_ref
  1.4 0.0 copy-start
  1.4 2.2 %copy-done = f32[2,8,256,256]{3,2,1,0:T(8,128)S(1)} copy-done((f32[2,8,256,256]{3,2,1,0:T(8,128)S(1)}, f32[2,8,256,256]{3,2,1,0:T(8,128)}, u32[]{:S(2)}) %copy-start) | copy-done | bytes 4194328
  3.6 0.0 copy-start.1
  3.6 2.2 %copy-done.1 = f32[2,8,256,256]{3,2,1,0:T(8,128)S(1)} copy-done((f32[2,8,256,256]{3,2,1,0:T(8,128)S(1)}, f32[2,8,256,256]{3,2,1,0:T(8,128)}, u32[]{:S(2)}) %copy-start.1) | copy-done | bytes 4194328
  5.8 0.0 copy-start.2
  5.8 1.1 copy-done.2
  6.9 0.0 copy-start.3
  6.9 1.1 copy-done.3
  8.1 13.2 %planes.1 = f32[32,2,2,8,8,256]{5,4,3,2,1,0:T(8,128)S(1)} custom-call(f32[2,8,256,256]{3,2,1,0:T(8,128)S(1)} %copy-done, f32[2,8,256,256]{3,2,1,0:T(8,128)S(1)} %copy-done, f32[2,8,256,256]{3,2,1,0:T(8,128)S(1)} %copy-done.1, f32[2,8,256,256]{3,2,1,0:T(8,128)S(1)} %copy-done.1, bf16[768,512]{1,0:T(8,128)(2,1)S(1)} %copy-done.3, ...), custom_call_target="tpu_custom_call" | custom-call | tf_op jit(solution)/shard_map/planes/pallas_call | solution.py:98
  21.3 105.9 %all_to_all.5 = f32[32,2,2,8,8,256]{5,4,3,2,1,0:T(8,128)} all-to-all(f32[32,2,2,8,8,256]{5,4,3,2,1,0:T(8,128)S(1)} %planes.1), channel_id=1, replica_groups=mesh['member'=4,'slab'=32] {'slab'}, dimensions={0} | all-to-all | bytes 16777216 | tf_op jit(solution)/shard_map/all_to_all | solution.py:209
  127.2 11.1 %sums.1 = f32[2,2,8,64,256]{4,3,2,1,0:T(8,128)S(1)} custom-call(s32[2]{0:T(128)S(1)} %pad_add_fusion.place_ref, f32[32,2,2,64,256]{4,3,2,1,0:T(8,128)} %bitcast.25, f32[32,2,2,64,256]{4,3,2,1,0:T(8,128)} %bitcast.26, f32[2,2,4,512,256]{4,3,2,1,0:T(8,128)} %bitcast.27, bf16[2,256,768]{2,1,0:T(8,128)(2,1)S(1)} %select_multiply_fusion.x_ref), custom_call_target="tpu_custom_call" | custom-call | tf_op jit(solution)/shard_map/sums/pallas_call | solution.py:164
  138.3 0.0 copy-start.4
  138.3 0.1 slice_bitcast_fusion
  138.4 2.8 %collective-permute-start = (f32[2,8,64,256]{3,2,1,0:T(8,128)S(1)}, f32[2,8,64,256]{3,2,1,0:T(8,128)S(1)}, u32[]{:S(2)}, u32[]{:S(2)}) collective-permute-start(f32[2,8,64,256]{3,2,1,0:T(8,128)S(1)} %slice_bitcast_fusion), channel_id=1, source_target_pairs={{0,32},{32,0},{64,96},{96,64},{1,33},{33,1},{65,97},{97,65},{2,34}... | collective-permute-start | bytes 3145736 | tf_op jit(solution)/shard_map/ppermute | solution.py:189
  141.2 2.3 %collective-permute-done = f32[2,8,64,256]{3,2,1,0:T(8,128)S(1)} collective-permute-done((f32[2,8,64,256]{3,2,1,0:T(8,128)S(1)}, f32[2,8,64,256]{3,2,1,0:T(8,128)S(1)}, u32[]{:S(2)}, u32[]{:S(2)}) %collective-permute-start) | collective-permute-done | bytes 1048608 | tf_op jit(solution)/shard_map/ppermute | solution.py:189
  143.5 0.1 fusion
  143.7 0.8 collective-permute-start.1
  144.5 12.4 %collective-permute-done.1 = f32[8,64,256]{2,1,0:T(8,128)S(1)} collective-permute-done((f32[8,64,256]{2,1,0:T(8,128)S(1)}, f32[8,64,256]{2,1,0:T(8,128)S(1)}, u32[]{:S(2)}, u32[]{:S(2)}) %collective-permute-start.1) | collective-permute-done | bytes 524320 | tf_op jit(solution)/shard_map/ppermute | solution.py:189
  156.9 0.0 copy-done.4
  156.9 0.3 fusion.3
  157.2 1.1 copy.10
  (1 shorter events, 0.0 us)
Async XLA Ops:
  1.4 2.2 %copy-start = (f32[2,8,256,256]{3,2,1,0:T(8,128)S(1)}, f32[2,8,256,256]{3,2,1,0:T(8,128)}, u32[]{:S(2)}) copy-start(f32[2,8,256,256]{3,2,1,0:T(8,128)} %right_ref.1) | copy-start | bytes 12582916
  3.6 2.2 %copy-start.1 = (f32[2,8,256,256]{3,2,1,0:T(8,128)S(1)}, f32[2,8,256,256]{3,2,1,0:T(8,128)}, u32[]{:S(2)}) copy-start(f32[2,8,256,256]{3,2,1,0:T(8,128)} %right_up_ref.1) | copy-start | bytes 12582916
  5.8 1.1 copy-start.2
  6.9 1.1 copy-start.3
  138.3 18.6 %copy-start.4 = (f32[64,8,256]{2,1,0:T(8,128)S(1)}, f32[64,8,256]{2,1,0:T(8,128)}, u32[]{:S(2)}) copy-start(f32[64,8,256]{2,1,0:T(8,128)} %param.11) | copy-start | bytes 1572868
  138.4 5.1 %collective-permute-start = (f32[2,8,64,256]{3,2,1,0:T(8,128)S(1)}, f32[2,8,64,256]{3,2,1,0:T(8,128)S(1)}, u32[]{:S(2)}, u32[]{:S(2)}) collective-permute-start(f32[2,8,64,256]{3,2,1,0:T(8,128)S(1)} %slice_bitcast_fusion), channel_id=1, source_target_pairs={{0,32},{32,0},{64,96},{96,64},{1,33},{33,1},{65,97},{97,65},{2,34}... | collective-permute-start | bytes 3145736 | tf_op jit(solution)/shard_map/ppermute | solution.py:189
  143.7 13.2 %collective-permute-start.1 = (f32[8,64,256]{2,1,0:T(8,128)S(1)}, f32[8,64,256]{2,1,0:T(8,128)S(1)}, u32[]{:S(2)}, u32[]{:S(2)}) collective-permute-start(f32[8,64,256]{2,1,0:T(8,128)S(1)} %slice_bitcast_fusion.2), channel_id=1, source_target_pairs={{0,64},{32,96},{64,0},{96,32},{1,65},{33,97},{65,1},{97,33},{2,66}... | collective-permute-start | bytes 1572872 | tf_op jit(solution)/shard_map/ppermute | solution.py:189

commit v2 on v0

v2 whole, which is shorter than its diff:
```python
import functools
import math

import jax
import jax.numpy as jnp
import ml_dtypes
import numpy as np
from jax import lax
from jax.experimental import pallas as pl
from jax.experimental.pallas import tpu as pltpu
from jax.sharding import PartitionSpec as P

sigmoid_slope = 8.0
grid_length = 256
half = grid_length // 2
devices_slab = 32
devices_member = 4


def waves(rows, columns):
    angles = (np.outer(rows, columns) % grid_length) * (2.0 * math.pi / grid_length)
    return np.cos(angles) / 16.0, -np.sin(angles) / 16.0


def split_table(table):
    high = table.astype(np.float32).astype(ml_dtypes.bfloat16)
    low = (table - high.astype(np.float64)).astype(np.float32).astype(ml_dtypes.bfloat16)
    return high, low


def along_z_table():
    real, imag = waves(np.arange(grid_length), np.arange(grid_length))
    high, low = split_table(np.concatenate((real, imag), axis=1))
    return np.concatenate((high, low), axis=0)


def stacked_table(real, imag):
    full = np.concatenate(
        (np.concatenate((real, -imag), axis=1), np.concatenate((imag, real), axis=1)), axis=0
    )
    return np.concatenate(split_table(full), axis=1)


def along_y_table():
    return np.stack(
        [
            stacked_table(*waves(np.arange(half), np.arange(parity, grid_length, 2)))
            for parity in range(2)
        ]
    )


def along_x_table():
    tables = []
    for core in range(2):
        order = np.concatenate(
            [np.arange(32) + 32 * (2 * z + c) for c in (1 - core, core) for z in range(2)]
        )
        tables.append(
            np.stack(
                [stacked_table(*waves(2 * order + parity, np.arange(half))) for parity in range(2)]
            )
        )
    return np.stack(tables)


def dot(left, right):
    return jnp.dot(left, right, preferred_element_type=jnp.float32)


def halve(values):
    high = values.astype(jnp.bfloat16)
    return high, (values - high.astype(jnp.float32)).astype(jnp.bfloat16)


def times(table, values):
    high, low = halve(values)
    return dot(table[:, :256], high) + dot(table[:, 256:], high) + dot(table[:, :256], low)


def planes_kernel(left_ref, right_ref, left_up_ref, right_up_ref, z_ref, y_ref, out_ref):
    count = left_ref.shape[1]

    def field_grad(plane, parity, structure_ref, upstream_ref):
        rows = pl.ds(parity, half, stride=2)
        structure = structure_ref[0, plane, rows, :]
        return upstream_ref[0, plane, rows, :] * sigmoid_slope * structure * (1.0 - structure)

    def after_z(plane):
        field = jnp.concatenate(
            [
                jnp.concatenate(
                    (
                        field_grad(plane, parity, left_ref, left_up_ref),
                        field_grad(plane, parity, right_ref, right_up_ref),
                    ),
                    axis=1,
                )
                for parity in range(2)
            ],
            axis=0,
        )
        high, low = halve(field)
        return dot(high, z_ref[0:256]) + dot(low, z_ref[0:256]) + dot(high, z_ref[256:512])

    def after_y(values):
        sums = []
        for parity in range(2):
            rows = values[parity * half : (parity + 1) * half]
            stacked = jnp.concatenate((rows[:, :grid_length], rows[:, grid_length:]), axis=0)
            sums.append(times(y_ref[parity], stacked))
        return sums[0] + sums[1], sums[0] - sums[1]

    def store(plane, below, above):
        for part in range(2):
            rows = slice(part * half, (part + 1) * half)
            for side in range(2):
                lanes = slice(side * 128, (side + 1) * 128)
                out_ref[:16, side, part, 0, plane] = below[rows, lanes].reshape(16, 8, 128)
                out_ref[16:, side, part, 0, plane] = above[rows, lanes].reshape(16, 8, 128)

    pending = after_z(0)
    done = None
    for plane in range(count):
        following = after_z(plane + 1) if plane + 1 < count else None
        results = after_y(pending)
        if done is not None:
            store(plane - 1, *done)
        pending, done = following, results
    store(count - 1, *done)


planes_per_step = 4


def planes(structure, upstream):
    members, depth = structure.shape[:2]
    blocks = [
        pl.BlockSpec(
            (1, planes_per_step, grid_length, 128), lambda m, x, side=side: (m, x, 0, side)
        )
        for side in range(2)
    ]
    return pl.pallas_call(
        planes_kernel,
        out_shape=jax.ShapeDtypeStruct(
            (devices_slab, 2, 2, members, depth, 8, 128), jnp.float32
        ),
        grid=(members, depth // planes_per_step),
        in_specs=[
            *blocks,
            *blocks,
            pl.BlockSpec((512, 512), lambda m, x: (0, 0)),
            pl.BlockSpec((2, 256, 512), lambda m, x: (0, 0, 0)),
        ],
        out_specs=pl.BlockSpec(
            (devices_slab, 2, 2, 1, planes_per_step, 8, 128),
            lambda m, x: (0, 0, 0, m, x, 0, 0),
        ),
        compiler_params=pltpu.CompilerParams(vmem_limit_bytes=60 * 1024 * 1024),
        name="planes",
    )(structure, structure, upstream, upstream, along_z_table(), along_y_table())


def sums_kernel(
    side, core_ref, received_ref, noise_ref, x_ref, give_ref, keep_ref
):
    members = received_ref.shape[3]
    core = core_ref[0]
    noise = noise_ref.reshape(2, members, 4, 1024, 128)

    def spectra(m, pair):
        def samples(first, part, k):
            block = received_ref[first : first + 16, side, part, m, pl.ds(k, 8, stride=8), :]
            return block.reshape(half, 128)

        def stacked(sign):
            return jnp.concatenate(
                [
                    jnp.concatenate(
                        [
                            samples(0, part, 2 * pair + k) + sign * samples(16, part, 2 * pair + k)
                            for k in range(2)
                        ],
                        axis=1,
                    )
                    for part in range(2)
                ],
                axis=0,
            )

        return [times(x_ref[core, parity], stacked(1 - 2 * parity)) for parity in range(2)]

    def weighted(m, pair, pieces):
        for parity in range(2):
            for c, out_ref in enumerate((give_ref, keep_ref)):
                for z in range(2):
                    block = 2 * z + jnp.bitwise_xor(core, 1 - c)
                    start = 64 * c + 32 * z
                    for k in range(2):
                        lanes = slice(k * 128, (k + 1) * 128)
                        y = 2 * pair + k
                        rows = pl.ds(16 * parity + 8 * side + y, 32, stride=32)
                        value = (
                            noise[0, m, block, rows, :] * pieces[parity][start : start + 32, lanes]
                            + noise[1, m, block, rows, :]
                            * pieces[parity][half + start : half + start + 32, lanes]
                        )
                        if m > 0:
                            value = value + out_ref[z, parity, y]
                        out_ref[z, parity, y] = value

    steps = [(m, pair) for m in range(members) for pair in range(4)]
    pieces = spectra(*steps[0])
    for i, (m, pair) in enumerate(steps):
        following = spectra(*steps[i + 1]) if i + 1 < len(steps) else None
        weighted(m, pair, pieces)
        pieces = following


def sums(side, received, noise, core):
    members = received.shape[3]
    out = jax.ShapeDtypeStruct((2, 2, 8, 32, 128), jnp.float32)
    vmem = pl.BlockSpec(memory_space=pltpu.VMEM)
    return pl.pallas_call(
        functools.partial(sums_kernel, side),
        out_shape=(out, out),
        in_specs=[
            pl.BlockSpec(memory_space=pltpu.SMEM),
            vmem,
            vmem,
            vmem,
        ],
        out_specs=(vmem, vmem),
        compiler_params=pltpu.CompilerParams(vmem_limit_bytes=24 * 1024 * 1024),
        name="sums",
    )(
        core,
        received.reshape(devices_slab, 2, 2, members, 64, 128),
        noise,
        along_x_table(),
    )


def density_kernel(z_ref, *refs):
    z = z_ref[0]
    density_ref, out_ref = refs[6], refs[7]
    density = density_ref.reshape(1024, 128)
    out = out_ref.reshape(1024, 128)
    for side in range(2):
        ours, chip, theirs = refs[3 * side : 3 * side + 3]
        for parity in range(2):
            for y in range(8):
                rows = pl.ds(16 * parity + 8 * side + y, 32, stride=32)
                total = ours[z, parity, y] + chip[z, parity, y] + theirs[parity, y]
                out[rows, :] = total / (2.0 * jnp.sqrt(density[rows, :]))


def tiles(values):
    values = values.reshape(values.shape[:-1] + (2, 128))
    return jnp.swapaxes(values, -3, -2)


def untiles(values):
    values = jnp.swapaxes(values, -3, -2)
    return values.reshape(values.shape[:-2] + (grid_length,))


def density_gradient(z_lo, pieces, density):
    vmem = pl.BlockSpec(memory_space=pltpu.VMEM)
    result = pl.pallas_call(
        density_kernel,
        out_shape=jax.ShapeDtypeStruct((64, 2, 8, 128), jnp.float32),
        in_specs=[pl.BlockSpec(memory_space=pltpu.SMEM)] + [vmem] * 7,
        out_specs=vmem,
        compiler_params=pltpu.CompilerParams(vmem_limit_bytes=8 * 1024 * 1024),
        name="density",
    )(z_lo, *pieces, tiles(density))
    return untiles(result)


def swap(values, flip):
    return lax.ppermute(values, "member", [(i, i ^ flip) for i in range(devices_member)])


def body(structure, upstream, noise, density):
    index = lax.axis_index("member").astype(jnp.int32)
    z_lo, core = index // 2, index % 2
    sent = planes(structure, upstream)
    sent, z_lo, core = lax.optimization_barrier((sent, z_lo, core))
    received = lax.all_to_all(sent, "slab", split_axis=0, concat_axis=0, tiled=True)
    received, z_lo, core = lax.optimization_barrier((received, z_lo, core))
    members = structure.shape[0]
    noise = tiles(noise).reshape(2, members, 4, 64, 2, 8, 128)
    pieces = []
    for side in range(2):
        give, keep = sums(side, received, noise, core.reshape(1))
        from_core = swap(give, 1)
        onward = lax.dynamic_index_in_dim(from_core, 1 - z_lo, 0, keepdims=False)
        onward = onward + lax.dynamic_index_in_dim(keep, 1 - z_lo, 0, keepdims=False)
        pieces += [keep, from_core, swap(onward, 2)]
    return density_gradient(z_lo.reshape(1), pieces, density)


def solution(mesh):
    in_specs = (
        P("member", "slab", None, None),
        P("member", "slab", None, None),
        P(None, "member", None, "slab", None),
        P("member", "slab", None),
    )
    out_specs = P("member", "slab", None)
    return jax.shard_map(body, mesh=mesh, in_specs=in_specs, out_specs=out_specs, check_vma=False)
```

time: 296 us -> 145 us (0.49); the launches traced: 293 us -> 145 us
  waiting for transfers between devices: 182 us -> 11.4 us
  blocking collectives: 0 us -> 106 us
  matrix products: 63.1 us -> 0 us
  Pallas kernels: 0 us -> 22.8 us
  local copies, waits for them, and re-layouts: 20.7 us -> 0.01 us
  between operations: 13.7 us -> 0.05 us
  starting transfers between devices: 11.3 us -> 4.44 us
    all_to_all x1 -> x0, waiting for transfers between devices: 146 us -> none  [body(): lax.all_to_all(planes, 'slab', split_axis=3, concat_axis=2, tiled=True)]
    all_to_all x0 -> x1, blocking collectives: none -> 106 us  [body(): lax.all_to_all(sent, 'slab', split_axis=0, concat_axis=0, tiled=True)]
    dot_general x10 -> x0, matrix products: 63.1 us -> none  [contract(): jnp.einsum(form, values, table, precision=lax.Precision.HIGHEST, preferre...]
    reduce_scatter x1 -> x0, waiting for transfers between devices: 35.4 us -> none  [body(): lax.psum_scatter(local_sum, 'member', scatter_dimension=0, tiled=True)]
    pallas_call x0 -> x4, Pallas kernels: none -> 22.8 us  [the longest x1 11.5 us: planes(): pl.pallas_call(planes_kernel, out_shape=jax.ShapeDtypeStruct((devices_sla...]
    ppermute x0 -> x4, waiting for transfers between devices: none -> 11.4 us  [swap(): lax.ppermute(values, 'member', [(i, i ^ flip) for i in range(devices_memb...]
    all_to_all x1 -> x0, starting transfers between devices: 11.3 us -> none  [body(): lax.all_to_all(planes, 'slab', split_axis=3, concat_axis=2, tiled=True)]
    another operation x1 -> x0, local copies, waits for them, and re-layouts: 8.08 us -> none  [body(): planes = jnp.stack((after_y_real, after_y_imag))]
  transfers between devices with their start and end apart: 2 -> 4, of which waited for: 2 -> 3; matrix products, arithmetic and copies ran while one was open for 2% -> 0% of each run, Pallas kernels for 0% -> 3%
where the time goes in v2:
time: 145 us
  blocking collectives  106 us (73%)
  Pallas kernels  22.8 us (16%)
  waiting for transfers between devices  11.4 us (8%)
  starting transfers between devices  4.44 us (3%)
    all_to_all x1, blocking collectives, body(): lax.all_to_all(sent, 'slab', split_axis=0, concat_axis=0, tiled=True)  106 us
    pallas_call x1, Pallas kernels, planes(): pl.pallas_call(planes_kernel, out_shape=jax.ShapeDtypeStruct((devices_sla...  11.5 us
    ppermute x4, waiting for transfers between devices, swap(): lax.ppermute(values, 'member', [(i, i ^ flip) for i in range(devices_memb...  11.4 us
    pallas_call x2, Pallas kernels, sums(): pl.pallas_call(functools.partial(sums_kernel, side), out_shape=(out, out)...  9.81 us
    ppermute x4, starting transfers between devices, swap(): lax.ppermute(values, 'member', [(i, i ^ flip) for i in range(devices_memb...  4.44 us
  transfers between devices with their start and end apart: 4, of which 3 were waited for; matrix products, arithmetic and copies ran while one was open for 0% of the time, Pallas kernels for 3%

profile of v2, /device:TPU:1, one launch (start us, length us, event | category | flops | bytes accessed | tf_op | source)
XLA Modules:
  0.0 145.1 jit_solution(2298067198255604864)
XLA Ops:
  0.0 11.5 %planes.1 = f32[32,2,2,2,8,8,128]{6,5,4,3,2,1,0:T(8,128)} custom-call(f32[2,8,256,256]{3,2,1,0:T(8,128)} %right_ref.1, f32[2,8,256,256]{3,2,1,0:T(8,128)} %right_ref.1, f32[2,8,256,256]{3,2,1,0:T(8,128)} %right_up_ref.1, f32[2,8,256,256]{3,2,1,0:T(8,128)} %right_up_ref.1, bf16[512,512]{1,0:T(8,128)(2,1)} %constant.49.clone.z_ref, ...), custom_call_target="tpu_custom_call" | custom-call | tf_op jit(solution)/shard_map/planes/pallas_call | solution.py:144
  11.5 0.0 copy-start
  11.5 0.0 copy-start.1
  11.5 106.3 %all_to_all.5 = f32[32,2,2,2,8,8,128]{6,5,4,3,2,1,0:T(8,128)S(1)} all-to-all(f32[32,2,2,2,8,8,128]{6,5,4,3,2,1,0:T(8,128)} %planes.1), channel_id=1, replica_groups=mesh['member'=4,'slab'=32] {'slab'}, dimensions={0} | all-to-all | bytes 16777216 | tf_op jit(solution)/shard_map/all_to_all | solution.py:291
  117.8 0.0 copy-done
  117.8 0.0 copy-done.1
  117.8 5.3 %sums.3 = (f32[2,2,8,32,128]{4,3,2,1,0:T(8,128)}, f32[2,2,8,32,128]{4,3,2,1,0:T(8,128)S(1)}) custom-call(s32[1]{0:T(128)} %bitcast.1.core_ref, f32[32,2,2,2,64,128]{5,4,3,2,1,0:T(8,128)S(1)} %bitcast.18, f32[2,2,4,64,2,8,128]{6,5,4,3,2,1,0:T(8,128)S(1)} %bitcast.20, bf16[2,2,256,512]{3,2,1,0:T(8,128)(2,1)S(1)} %copy-done.1), custom_call_target="tpu_custom_call" | custom-call | tf_op jit(solution)/shard_map/sums/pallas_call | solution.py:225
  123.1 0.0 copy-start.2
  123.1 2.7 %collective-permute-start.2 = (f32[2,2,8,32,128]{4,3,2,1,0:T(8,128)}, f32[2,2,8,32,128]{4,3,2,1,0:T(8,128)S(1)}, u32[]{:S(2)}, u32[]{:S(2)}) collective-permute-start(f32[2,2,8,32,128]{4,3,2,1,0:T(8,128)} %get-tuple-element.24), channel_id=1, source_target_pairs={{0,32},{32,0},{64,96},{96,64},{1,33},{33,1},{65,97},{97,65},{2,34}... | collective-permute-start | bytes 1572872 | tf_op jit(solution)/shard_map/ppermute | solution.py:283
  125.8 4.6 %sums.2 = (f32[2,2,8,32,128]{4,3,2,1,0:T(8,128)S(1)}, f32[2,2,8,32,128]{4,3,2,1,0:T(8,128)S(1)}) custom-call(s32[1]{0:T(128)} %bitcast.1.core_ref, f32[32,2,2,2,64,128]{5,4,3,2,1,0:T(8,128)S(1)} %bitcast.19, f32[2,2,4,64,2,8,128]{6,5,4,3,2,1,0:T(8,128)S(1)} %bitcast.21, bf16[2,2,256,512]{3,2,1,0:T(8,128)(2,1)S(1)} %copy-done.1), custom_call_target="tpu_custom_call" | custom-call | tf_op jit(solution)/shard_map/sums/pallas_call | solution.py:225
  130.4 0.1 collective-permute-start
  130.5 0.0 collective-permute-done.2.refs_4_
  130.5 0.8 collective-permute-start.3
  131.3 1.0 collective-permute-done.refs_1_
  132.4 0.8 collective-permute-start.1
  133.2 4.8 %collective-permute-done.3.refs_5_ = f32[2,8,32,128]{3,2,1,0:T(8,128)S(1)} collective-permute-done((f32[2,8,32,128]{3,2,1,0:T(8,128)S(1)}, f32[2,8,32,128]{3,2,1,0:T(8,128)S(1)}, u32[]{:S(2)}, u32[]{:S(2)}) %collective-permute-start.3) | collective-permute-done | bytes 262176 | tf_op jit(solution)/shard_map/ppermute | solution.py:283
  138.0 5.6 %collective-permute-done.1.refs_2_ = f32[2,8,32,128]{3,2,1,0:T(8,128)S(1)} collective-permute-done((f32[2,8,32,128]{3,2,1,0:T(8,128)S(1)}, f32[2,8,32,128]{3,2,1,0:T(8,128)S(1)}, u32[]{:S(2)}, u32[]{:S(2)}) %collective-permute-start.1) | collective-permute-done | bytes 262176 | tf_op jit(solution)/shard_map/ppermute | solution.py:283
  143.6 0.0 copy-done.2
  143.6 1.5 %density.1 = f32[64,2,8,128]{3,2,1,0:T(8,128)} custom-call(s32[1]{0:T(128)} %bitcast.z_ref, f32[2,2,8,32,128]{4,3,2,1,0:T(8,128)S(1)} %get-tuple-element.21.refs_0_, f32[2,2,8,32,128]{4,3,2,1,0:T(8,128)S(1)} %collective-permute-done.refs_1_, f32[2,8,32,128]{3,2,1,0:T(8,128)S(1)} %collective-permute-done.1.refs_2_, ...), custom_call_target="tpu_custom_call" | custom-call | tf_op jit(solution)/shard_map/density/pallas_call | solution.py:271
  (2 shorter events, 0.1 us)
Async XLA Ops:
  11.5 106.3 %copy-start = (f32[2,2,256,8,256]{4,3,2,1,0:T(8,128)S(1)}, f32[2,2,256,8,256]{4,3,2,1,0:T(8,128)}, u32[]{:S(2)}) copy-start(f32[2,2,256,8,256]{4,3,2,1,0:T(8,128)} %param.10) | copy-start | bytes 25165828
  11.5 106.3 %copy-start.1 = (bf16[2,2,256,512]{3,2,1,0:T(8,128)(2,1)S(1)}, bf16[2,2,256,512]{3,2,1,0:T(8,128)(2,1)}, u32[]{:S(2)}) copy-start(bf16[2,2,256,512]{3,2,1,0:T(8,128)(2,1)} %constant.51.clone.x_ref) | copy-start | bytes 3145732
  123.1 20.5 %copy-start.2 = (f32[64,8,256]{2,1,0:T(8,128)S(1)}, f32[64,8,256]{2,1,0:T(8,128)}, u32[]{:S(2)}) copy-start(f32[64,8,256]{2,1,0:T(8,128)} %param.11) | copy-start | bytes 1572868
  123.1 7.4 %collective-permute-start.2 = (f32[2,2,8,32,128]{4,3,2,1,0:T(8,128)}, f32[2,2,8,32,128]{4,3,2,1,0:T(8,128)S(1)}, u32[]{:S(2)}, u32[]{:S(2)}) collective-permute-start(f32[2,2,8,32,128]{4,3,2,1,0:T(8,128)} %get-tuple-element.24), channel_id=1, source_target_pairs={{0,32},{32,0},{64,96},{96,64},{1,33},{33,1},{65,97},{97,65},{2,34}... | collective-permute-start | bytes 1572872 | tf_op jit(solution)/shard_map/ppermute | solution.py:283
  130.4 2.0 %collective-permute-start = (f32[2,2,8,32,128]{4,3,2,1,0:T(8,128)S(1)}, f32[2,2,8,32,128]{4,3,2,1,0:T(8,128)S(1)}, u32[]{:S(2)}, u32[]{:S(2)}) collective-permute-start(f32[2,2,8,32,128]{4,3,2,1,0:T(8,128)S(1)} %get-tuple-element.22), channel_id=1, source_target_pairs={{0,32},{32,0},{64,96},{96,64},{1,33},{33,1},{65,97},{97,65},{2,34}... | collective-permute-start | bytes 1572872 | tf_op jit(solution)/shard_map/ppermute | solution.py:283
  130.5 7.5 %collective-permute-start.3 = (f32[2,8,32,128]{3,2,1,0:T(8,128)S(1)}, f32[2,8,32,128]{3,2,1,0:T(8,128)S(1)}, u32[]{:S(2)}, u32[]{:S(2)}) collective-permute-start(f32[2,8,32,128]{3,2,1,0:T(8,128)S(1)} %add_bitcast_fusion), channel_id=1, source_target_pairs={{0,64},{32,96},{64,0},{96,32},{1,65},{33,97},{65,1},{97,33},{2,66}... | collective-permute-start | bytes 786440 | tf_op jit(solution)/shard_map/ppermute | solution.py:283
  132.4 11.2 %collective-permute-start.1 = (f32[2,8,32,128]{3,2,1,0:T(8,128)S(1)}, f32[2,8,32,128]{3,2,1,0:T(8,128)S(1)}, u32[]{:S(2)}, u32[]{:S(2)}) collective-permute-start(f32[2,8,32,128]{3,2,1,0:T(8,128)S(1)} %add_bitcast_fusion.1), channel_id=1, source_target_pairs={{0,64},{32,96},{64,0},{96,32},{1,65},{33,97},{65,1},{97,33},{2,66}... | collective-permute-start | bytes 786440 | tf_op jit(solution)/shard_map/ppermute | solution.py:283

commit v3 on v2

--- a/solution.py
+++ b/solution.py
@@ -51,17 +51,17 @@
 
 
 def along_x_table():
-    tables = []
-    for core in range(2):
-        order = np.concatenate(
-            [np.arange(32) + 32 * (2 * z + c) for c in (1 - core, core) for z in range(2)]
-        )
-        tables.append(
+    return np.stack(
+        [
             np.stack(
-                [stacked_table(*waves(2 * order + parity, np.arange(half))) for parity in range(2)]
+                [
+                    stacked_table(*waves(2 * np.arange(32 * i, 32 * i + 32) + parity, np.arange(half)))
+                    for parity in range(2)
+                ]
             )
-        )
-    return np.stack(tables)
+            for i in range(devices_member)
+        ]
+    )
 
 
 def dot(left, right):
@@ -162,14 +162,17 @@
     )(structure, structure, upstream, upstream, along_z_table(), along_y_table())
 
 
-def sums_kernel(
-    side, core_ref, received_ref, noise_ref, x_ref, give_ref, keep_ref
-):
+def sums_kernel(sides, place_ref, received_ref, noise_ref, x_ref, give_ref, keep_ref):
     members = received_ref.shape[3]
-    core = core_ref[0]
-    noise = noise_ref.reshape(2, members, 4, 1024, 128)
-
-    def spectra(m, pair):
+    noise = noise_ref.reshape(2, members, devices_member, 1024, 128)
+    give, keep = 2 * place_ref[0] + 1 - place_ref[1], 2 * place_ref[0] + place_ref[1]
+    outputs = ((give, give_ref), (keep, keep_ref))
+    tables = [
+        jnp.concatenate([x_ref[block, parity] for block, _ in outputs], axis=0)
+        for parity in range(2)
+    ]
+
+    def spectra(side, m, pair):
         def samples(first, part, k):
             block = received_ref[first : first + 16, side, part, m, pl.ds(k, 8, stride=8), :]
             return block.reshape(half, 128)
@@ -189,73 +192,59 @@
                 axis=0,
             )
 
-        return [times(x_ref[core, parity], stacked(1 - 2 * parity)) for parity in range(2)]
-
-    def weighted(m, pair, pieces):
+        return [times(tables[parity], stacked(1 - 2 * parity)) for parity in range(2)]
+
+    def weighted(side, m, pair, pieces, earlier):
+        values = {}
         for parity in range(2):
-            for c, out_ref in enumerate((give_ref, keep_ref)):
-                for z in range(2):
-                    block = 2 * z + jnp.bitwise_xor(core, 1 - c)
-                    start = 64 * c + 32 * z
-                    for k in range(2):
-                        lanes = slice(k * 128, (k + 1) * 128)
-                        y = 2 * pair + k
-                        rows = pl.ds(16 * parity + 8 * side + y, 32, stride=32)
-                        value = (
-                            noise[0, m, block, rows, :] * pieces[parity][start : start + 32, lanes]
-                            + noise[1, m, block, rows, :]
-                            * pieces[parity][half + start : half + start + 32, lanes]
-                        )
-                        if m > 0:
-                            value = value + out_ref[z, parity, y]
-                        out_ref[z, parity, y] = value
-
-    steps = [(m, pair) for m in range(members) for pair in range(4)]
-    pieces = spectra(*steps[0])
-    for i, (m, pair) in enumerate(steps):
-        following = spectra(*steps[i + 1]) if i + 1 < len(steps) else None
-        weighted(m, pair, pieces)
-        pieces = following
-
-
-def sums(side, received, noise, core):
+            for i, (block, _) in enumerate(outputs):
+                for k in range(2):
+                    lanes = slice(k * 128, (k + 1) * 128)
+                    y = 2 * pair + k
+                    rows = pl.ds(16 * parity + 8 * side + y, 32, stride=32)
+                    value = (
+                        noise[0, m, block, rows, :] * pieces[parity][64 * i : 64 * i + 32, lanes]
+                        + noise[1, m, block, rows, :]
+                        * pieces[parity][64 * i + 32 : 64 * i + 64, lanes]
+                    )
+                    key = (i, parity, y)
+                    values[key] = value + earlier[key] if earlier else value
+        return values
+
+    for position, side in enumerate(sides):
+        for pair in range(4):
+            values = None
+            for m in range(members):
+                values = weighted(side, m, pair, spectra(side, m, pair), values)
+            for (i, parity, y), value in values.items():
+                rows = pl.ds(8 * parity + y, 32, stride=16)
+                outputs[i][1].at[position].reshape(512, 128)[rows, :] = value
+
+
+def sums(sides, received, noise, place):
     members = received.shape[3]
-    out = jax.ShapeDtypeStruct((2, 2, 8, 32, 128), jnp.float32)
+    out = jax.ShapeDtypeStruct((len(sides), 64, 8, 128), jnp.float32)
     vmem = pl.BlockSpec(memory_space=pltpu.VMEM)
     return pl.pallas_call(
-        functools.partial(sums_kernel, side),
+        functools.partial(sums_kernel, sides),
         out_shape=(out, out),
-        in_specs=[
-            pl.BlockSpec(memory_space=pltpu.SMEM),
-            vmem,
-            vmem,
-            vmem,
-        ],
+        in_specs=[pl.BlockSpec(memory_space=pltpu.SMEM), vmem, vmem, vmem],
         out_specs=(vmem, vmem),
         compiler_params=pltpu.CompilerParams(vmem_limit_bytes=24 * 1024 * 1024),
+        cost_estimate=pl.CostEstimate(
+            flops=len(sides) * 6 * members * 16 * 128 * 256 * 256,
+            bytes_accessed=len(sides) * 16 * 1024 * 1024,
+            transcendentals=0,
+        ),
         name="sums",
     )(
-        core,
+        place,
         received.reshape(devices_slab, 2, 2, members, 64, 128),
         noise,
         along_x_table(),
     )
 
 
-def density_kernel(z_ref, *refs):
-    z = z_ref[0]
-    density_ref, out_ref = refs[6], refs[7]
-    density = density_ref.reshape(1024, 128)
-    out = out_ref.reshape(1024, 128)
-    for side in range(2):
-        ours, chip, theirs = refs[3 * side : 3 * side + 3]
-        for parity in range(2):
-            for y in range(8):
-                rows = pl.ds(16 * parity + 8 * side + y, 32, stride=32)
-                total = ours[z, parity, y] + chip[z, parity, y] + theirs[parity, y]
-                out[rows, :] = total / (2.0 * jnp.sqrt(density[rows, :]))
-
-
 def tiles(values):
     values = values.reshape(values.shape[:-1] + (2, 128))
     return jnp.swapaxes(values, -3, -2)
@@ -266,19 +255,6 @@
     return values.reshape(values.shape[:-2] + (grid_length,))
 
 
-def density_gradient(z_lo, pieces, density):
-    vmem = pl.BlockSpec(memory_space=pltpu.VMEM)
-    result = pl.pallas_call(
-        density_kernel,
-        out_shape=jax.ShapeDtypeStruct((64, 2, 8, 128), jnp.float32),
-        in_specs=[pl.BlockSpec(memory_space=pltpu.SMEM)] + [vmem] * 7,
-        out_specs=vmem,
-        compiler_params=pltpu.CompilerParams(vmem_limit_bytes=8 * 1024 * 1024),
-        name="density",
-    )(z_lo, *pieces, tiles(density))
-    return untiles(result)
-
-
 def swap(values, flip):
     return lax.ppermute(values, "member", [(i, i ^ flip) for i in range(devices_member)])
 
@@ -286,20 +262,23 @@
 def body(structure, upstream, noise, density):
     index = lax.axis_index("member").astype(jnp.int32)
     z_lo, core = index // 2, index % 2
+    ours, theirs = jnp.stack((z_lo, core)), jnp.stack((1 - z_lo, core))
     sent = planes(structure, upstream)
-    sent, z_lo, core = lax.optimization_barrier((sent, z_lo, core))
+    sent, ours, theirs = lax.optimization_barrier((sent, ours, theirs))
     received = lax.all_to_all(sent, "slab", split_axis=0, concat_axis=0, tiled=True)
-    received, z_lo, core = lax.optimization_barrier((received, z_lo, core))
-    members = structure.shape[0]
-    noise = tiles(noise).reshape(2, members, 4, 64, 2, 8, 128)
-    pieces = []
+    received, ours, theirs = lax.optimization_barrier((received, ours, theirs))
+    noise = tiles(noise).reshape(2, structure.shape[0], devices_member, 64, 2, 8, 128)
+    crossing = []
     for side in range(2):
-        give, keep = sums(side, received, noise, core.reshape(1))
-        from_core = swap(give, 1)
-        onward = lax.dynamic_index_in_dim(from_core, 1 - z_lo, 0, keepdims=False)
-        onward = onward + lax.dynamic_index_in_dim(keep, 1 - z_lo, 0, keepdims=False)
-        pieces += [keep, from_core, swap(onward, 2)]
-    return density_gradient(z_lo.reshape(1), pieces, density)
+        give, keep = sums((side,), received, noise, theirs)
+        crossing.append(swap(give, 1) + keep)
+    crossing = jnp.concatenate(crossing)
+    arrived = swap(crossing, 2)
+    ours, _ = lax.optimization_barrier((ours, crossing))
+    give, keep = sums((0, 1), received, noise, ours)
+    chip = jnp.concatenate([swap(give[side : side + 1], 1) for side in range(2)])
+    total = keep + chip + arrived
+    return untiles(jnp.swapaxes(total, 0, 1) / (2.0 * jnp.sqrt(tiles(density))))
 
 
 def solution(mesh):

time: 145 us -> 144 us (level)
  waiting for transfers between devices: 11.4 us -> 7.45 us
    ppermute x4 -> x5, waiting for transfers between devices: 11.4 us -> 7.45 us  [swap(): lax.ppermute(values, 'member', [(i, i ^ flip) for i in range(devices_memb...]
    ppermute x4 -> x5, starting transfers between devices: 4.44 us -> 4.49 us  [swap(): lax.ppermute(values, 'member', [(i, i ^ flip) for i in range(devices_memb...]
  transfers between devices with their start and end apart: 4 -> 5, of which waited for: 3 -> 4; matrix products, arithmetic and copies ran while one was open for 0% -> 0% of each run, Pallas kernels for 3% -> 6%
where the time goes in v3:
time: 144 us
  blocking collectives  106 us (74%)
  Pallas kernels  24 us (17%)
  waiting for transfers between devices  7.45 us (5%)
  starting transfers between devices  4.49 us (3%)
    all_to_all x1, blocking collectives, body(): lax.all_to_all(sent, 'slab', split_axis=0, concat_axis=0, tiled=True)  106 us
    pallas_call x3, Pallas kernels, sums(): pl.pallas_call(functools.partial(sums_kernel, sides), out_shape=(out, out...  12.6 us
    pallas_call x1, Pallas kernels, planes(): pl.pallas_call(planes_kernel, out_shape=jax.ShapeDtypeStruct((devices_sla...  11.5 us
    ppermute x5, waiting for transfers between devices, swap(): lax.ppermute(values, 'member', [(i, i ^ flip) for i in range(devices_memb...  7.45 us
    ppermute x5, starting transfers between devices, swap(): lax.ppermute(values, 'member', [(i, i ^ flip) for i in range(devices_memb...  4.49 us
  transfers between devices with their start and end apart: 5, of which 4 were waited for; matrix products, arithmetic and copies ran while one was open for 0% of the time, Pallas kernels for 6%

profile of v3, /device:TPU:1, one launch (start us, length us, event | category | flops | bytes accessed | tf_op | source)
XLA Modules:
  0.0 143.6 jit_solution(139380539584781623)
XLA Ops:
  0.0 0.1 pad_add_fusion
  0.1 11.5 %planes.1 = f32[32,2,2,2,8,8,128]{6,5,4,3,2,1,0:T(8,128)} custom-call(f32[2,8,256,256]{3,2,1,0:T(8,128)} %right_ref.1, f32[2,8,256,256]{3,2,1,0:T(8,128)} %right_ref.1, f32[2,8,256,256]{3,2,1,0:T(8,128)} %right_up_ref.1, f32[2,8,256,256]{3,2,1,0:T(8,128)} %right_up_ref.1, bf16[512,512]{1,0:T(8,128)(2,1)} %constant.39.clone.z_ref, ...), custom_call_target="tpu_custom_call" | custom-call | tf_op jit(solution)/shard_map/planes/pallas_call | solution.py:144
  11.6 0.0 copy-start
  11.6 0.0 copy-start.1
  11.6 106.3 %all_to_all.5 = f32[32,2,2,2,8,8,128]{6,5,4,3,2,1,0:T(8,128)S(1)} all-to-all(f32[32,2,2,2,8,8,128]{6,5,4,3,2,1,0:T(8,128)} %planes.1), channel_id=1, replica_groups=mesh['member'=4,'slab'=32] {'slab'}, dimensions={0} | all-to-all | bytes 16777216 | tf_op jit(solution)/shard_map/all_to_all | solution.py:268
  117.9 0.0 copy-done
  117.9 0.0 copy-done.1
  117.9 3.3 %sums.4 = (f32[1,64,8,128]{3,2,1,0:T(8,128)S(1)}, f32[1,64,8,128]{3,2,1,0:T(8,128)S(1)}) custom-call(s32[2]{0:T(128)S(1)} %get-tuple-element.22.place_ref, f32[32,2,2,2,64,128]{5,4,3,2,1,0:T(8,128)S(1)} %bitcast.20, f32[2,2,4,64,2,8,128]{6,5,4,3,2,1,0:T(8,128)S(1)} %bitcast.23, bf16[4,2,64,512]{3,2,1,0:T(8,128)(2,1)S(1)} %copy-done.1), custom_call_target="tpu_custom_call" | custom-call | flops 1610612736 | bytes 16777216 | tf_op jit(solution)/shard_map/sums/pallas_call | solution.py:228
  121.2 2.8 %collective-permute-start.1 = (f32[1,64,8,128]{3,2,1,0:T(8,128)S(1)}, f32[1,64,8,128]{3,2,1,0:T(8,128)S(1)}, u32[]{:S(2)}, u32[]{:S(2)}) collective-permute-start(f32[1,64,8,128]{3,2,1,0:T(8,128)S(1)} %get-tuple-element.26), channel_id=1, source_target_pairs={{0,32},{32,0},{64,96},{96,64},{1,33},{33,1},{65,97},{97,65},{2,34}... | collective-permute-start | bytes 786440 | tf_op jit(solution)/shard_map/ppermute | solution.py:259
  124.0 3.3 %sums.3 = (f32[1,64,8,128]{3,2,1,0:T(8,128)S(1)}, f32[1,64,8,128]{3,2,1,0:T(8,128)S(1)}) custom-call(s32[2]{0:T(128)S(1)} %get-tuple-element.22.place_ref, f32[32,2,2,2,64,128]{5,4,3,2,1,0:T(8,128)S(1)} %bitcast.21, f32[2,2,4,64,2,8,128]{6,5,4,3,2,1,0:T(8,128)S(1)} %bitcast.24, bf16[4,2,64,512]{3,2,1,0:T(8,128)(2,1)S(1)} %copy-done.1), custom_call_target="tpu_custom_call" | custom-call | flops 1610612736 | bytes 16777216 | tf_op jit(solution)/shard_map/sums/pallas_call | solution.py:228
  127.2 0.1 collective-permute-start
  127.3 0.0 collective-permute-done.1
  127.4 1.5 %collective-permute-done = f32[1,64,8,128]{3,2,1,0:T(8,128)S(1)} collective-permute-done((f32[1,64,8,128]{3,2,1,0:T(8,128)S(1)}, f32[1,64,8,128]{3,2,1,0:T(8,128)S(1)}, u32[]{:S(2)}, u32[]{:S(2)}) %collective-permute-start) | collective-permute-done | bytes 262176 | tf_op jit(solution)/shard_map/ppermute | solution.py:259
  128.9 0.0 copy-start.2
  128.9 1.0 collective-permute-start.4
  129.9 6.0 %sums.5 = (f32[2,64,8,128]{3,2,1,0:T(8,128)S(1)}, f32[2,64,8,128]{3,2,1,0:T(8,128)S(1)}) custom-call(s32[2]{0:T(128)S(1)} %get-tuple-element.28.place_ref, f32[32,2,2,2,64,128]{5,4,3,2,1,0:T(8,128)S(1)} %bitcast.22, f32[2,2,4,64,2,8,128]{6,5,4,3,2,1,0:T(8,128)S(1)} %bitcast.25, bf16[4,2,64,512]{3,2,1,0:T(8,128)(2,1)S(1)} %copy-done.1), custom_call_target="tpu_custom_call" | custom-call | flops 3221225472 | bytes 33554432 | tf_op jit(solution)/shard_map/sums/pallas_call | solution.py:228
  136.0 0.5 collective-permute-start.2
  136.5 0.1 collective-permute-start.3
  136.6 1.1 collective-permute-done.2
  137.7 0.4 collective-permute-done.3
  138.1 4.5 %collective-permute-done.4 = f32[2,64,8,128]{3,2,1,0:T(8,128)S(1)} collective-permute-done((f32[2,64,8,128]{3,2,1,0:T(8,128)S(1)}, f32[2,64,8,128]{3,2,1,0:T(8,128)S(1)}, u32[]{:S(2)}, u32[]{:S(2)}) %collective-permute-start.4) | collective-permute-done | bytes 524320 | tf_op jit(solution)/shard_map/ppermute | solution.py:259
  142.6 0.0 copy-done.2
  142.6 1.0 copy_bitcast_fusion
  (4 shorter events, 0.1 us)
Async XLA Ops:
  11.6 106.3 %copy-start = (f32[2,2,256,8,256]{4,3,2,1,0:T(8,128)S(1)}, f32[2,2,256,8,256]{4,3,2,1,0:T(8,128)}, u32[]{:S(2)}) copy-start(f32[2,2,256,8,256]{4,3,2,1,0:T(8,128)} %param.11) | copy-start | bytes 25165828
  11.6 106.3 %copy-start.1 = (bf16[4,2,64,512]{3,2,1,0:T(8,128)(2,1)S(1)}, bf16[4,2,64,512]{3,2,1,0:T(8,128)(2,1)}, u32[]{:S(2)}) copy-start(bf16[4,2,64,512]{3,2,1,0:T(8,128)(2,1)} %constant.41.clone.x_ref) | copy-start | bytes 1572868
  121.2 6.2 %collective-permute-start.1 = (f32[1,64,8,128]{3,2,1,0:T(8,128)S(1)}, f32[1,64,8,128]{3,2,1,0:T(8,128)S(1)}, u32[]{:S(2)}, u32[]{:S(2)}) collective-permute-start(f32[1,64,8,128]{3,2,1,0:T(8,128)S(1)} %get-tuple-element.26), channel_id=1, source_target_pairs={{0,32},{32,0},{64,96},{96,64},{1,33},{33,1},{65,97},{97,65},{2,34}... | collective-permute-start | bytes 786440 | tf_op jit(solution)/shard_map/ppermute | solution.py:259
  127.2 1.6 %collective-permute-start = (f32[1,64,8,128]{3,2,1,0:T(8,128)S(1)}, f32[1,64,8,128]{3,2,1,0:T(8,128)S(1)}, u32[]{:S(2)}, u32[]{:S(2)}) collective-permute-start(f32[1,64,8,128]{3,2,1,0:T(8,128)S(1)} %get-tuple-element.24), channel_id=1, source_target_pairs={{0,32},{32,0},{64,96},{96,64},{1,33},{33,1},{65,97},{97,65},{2,34}... | collective-permute-start | bytes 786440 | tf_op jit(solution)/shard_map/ppermute | solution.py:259
  128.9 13.7 %copy-start.2 = (f32[64,8,256]{2,1,0:T(8,128)S(1)}, f32[64,8,256]{2,1,0:T(8,128)}, u32[]{:S(2)}) copy-start(f32[64,8,256]{2,1,0:T(8,128)} %param.12) | copy-start | bytes 1572868
  128.9 13.6 %collective-permute-start.4 = (f32[2,64,8,128]{3,2,1,0:T(8,128)S(1)}, f32[2,64,8,128]{3,2,1,0:T(8,128)S(1)}, u32[]{:S(2)}, u32[]{:S(2)}) collective-permute-start(f32[2,64,8,128]{3,2,1,0:T(8,128)S(1)} %pad_maximum_fusion), channel_id=1, source_target_pairs={{0,64},{32,96},{64,0},{96,32},{1,65},{33,97},{65,1},{97,33},{2,66}... | collective-permute-start | bytes 1572872 | tf_op jit(solution)/shard_map/ppermute | solution.py:259
  136.0 1.7 %collective-permute-start.2 = (f32[1,64,8,128]{3,2,1,0:T(8,128)S(1)}, f32[1,64,8,128]{3,2,1,0:T(8,128)S(1)}, u32[]{:S(2)}, u32[]{:S(2)}) collective-permute-start(f32[1,64,8,128]{3,2,1,0:T(8,128)S(1)} %get-tuple-element.31), channel_id=1, source_target_pairs={{0,32},{32,0},{64,96},{96,64},{1,33},{33,1},{65,97},{97,65},{2,34}... | collective-permute-start | bytes 786440 | tf_op jit(solution)/shard_map/ppermute | solution.py:259
  136.5 1.5 %collective-permute-start.3 = (f32[1,64,8,128]{3,2,1,0:T(8,128)S(1)}, f32[1,64,8,128]{3,2,1,0:T(8,128)S(1)}, u32[]{:S(2)}, u32[]{:S(2)}) collective-permute-start(f32[1,64,8,128]{3,2,1,0:T(8,128)S(1)} %get-tuple-element.32), channel_id=1, source_target_pairs={{0,32},{32,0},{64,96},{96,64},{1,33},{33,1},{65,97},{97,65},{2,34}... | collective-permute-start | bytes 786440 | tf_op jit(solution)/shard_map/ppermute | solution.py:259

commit v4 on v3

--- a/solution.py
+++ b/solution.py
@@ -29,8 +29,8 @@
 
 
 def along_z_table():
-    real, imag = waves(np.arange(grid_length), np.arange(grid_length))
-    high, low = split_table(np.concatenate((real, imag), axis=1))
+    real, imag = waves(np.arange(grid_length), np.arange(half + 1))
+    high, low = split_table(np.concatenate((real[:, :half], real[:, half:], imag[:, 1:half]), axis=1))
     return np.concatenate((high, low), axis=0)
 
 
@@ -101,7 +101,20 @@
             axis=0,
         )
         high, low = halve(field)
-        return dot(high, z_ref[0:256]) + dot(low, z_ref[0:256]) + dot(high, z_ref[256:512])
+        table_high, table_low = z_ref[0:256], z_ref[256:512]
+        raw = dot(high, table_high) + dot(low, table_high) + dot(high, table_low)
+        below_real, below_imag = raw[:, :half], raw[:, half:]
+        lane = lax.broadcasted_iota(jnp.int32, (grid_length, half), 1)
+        first = lane == 0
+        opposite = jnp.where(first, 0, half - lane)
+
+        def mirrored(values):
+            return jnp.take_along_axis(values, opposite, axis=1, mode="promise_in_bounds")
+
+        above_real = jnp.where(first, below_imag, mirrored(below_real))
+        above_imag = jnp.where(first, 0.0, -mirrored(below_imag))
+        below_imag = jnp.where(first, 0.0, below_imag)
+        return jnp.concatenate((below_real, above_real, below_imag, above_imag), axis=1)
 
     def after_y(values):
         sums = []
@@ -150,7 +163,7 @@
         in_specs=[
             *blocks,
             *blocks,
-            pl.BlockSpec((512, 512), lambda m, x: (0, 0)),
+            pl.BlockSpec((512, 256), lambda m, x: (0, 0)),
             pl.BlockSpec((2, 256, 512), lambda m, x: (0, 0, 0)),
         ],
         out_specs=pl.BlockSpec(
@@ -268,11 +281,8 @@
     received = lax.all_to_all(sent, "slab", split_axis=0, concat_axis=0, tiled=True)
     received, ours, theirs = lax.optimization_barrier((received, ours, theirs))
     noise = tiles(noise).reshape(2, structure.shape[0], devices_member, 64, 2, 8, 128)
-    crossing = []
-    for side in range(2):
-        give, keep = sums((side,), received, noise, theirs)
-        crossing.append(swap(give, 1) + keep)
-    crossing = jnp.concatenate(crossing)
+    give, keep = sums((0, 1), received, noise, theirs)
+    crossing = swap(give, 1) + keep
     arrived = swap(crossing, 2)
     ours, _ = lax.optimization_barrier((ours, crossing))
     give, keep = sums((0, 1), received, noise, ours)

time: 144 us -> 142 us (0.986)
    pallas_call x3 -> x2, Pallas kernels: 12.6 us -> 12 us  [sums(): pl.pallas_call(functools.partial(sums_kernel, sides), out_shape=(out, out...]
    ppermute x5 -> x4, waiting for transfers between devices: 7.45 us -> 7.03 us  [swap(): lax.ppermute(values, 'member', [(i, i ^ flip) for i in range(devices_memb...]
    ppermute x5 -> x4, starting transfers between devices: 4.49 us -> 4.62 us  [swap(): lax.ppermute(values, 'member', [(i, i ^ flip) for i in range(devices_memb...]
  transfers between devices with their start and end apart: 5 -> 4, of which waited for: 4 -> 4; matrix products, arithmetic and copies ran while one was open for 0% -> 0% of each run, Pallas kernels for 6% -> 4%
where the time goes in v4:
time: 142 us
  blocking collectives  106 us (75%)
  Pallas kernels  22.9 us (16%)
  waiting for transfers between devices  7.03 us (5%)
  starting transfers between devices  4.62 us (3%)
    all_to_all x1, blocking collectives, body(): lax.all_to_all(sent, 'slab', split_axis=0, concat_axis=0, tiled=True)  106 us
    pallas_call x2, Pallas kernels, sums(): pl.pallas_call(functools.partial(sums_kernel, sides), out_shape=(out, out...  12 us
    pallas_call x1, Pallas kernels, planes(): pl.pallas_call(planes_kernel, out_shape=jax.ShapeDtypeStruct((devices_sla...  10.8 us
    ppermute x4, waiting for transfers between devices, swap(): lax.ppermute(values, 'member', [(i, i ^ flip) for i in range(devices_memb...  7.03 us
    ppermute x4, starting transfers between devices, swap(): lax.ppermute(values, 'member', [(i, i ^ flip) for i in range(devices_memb...  4.62 us
  transfers between devices with their start and end apart: 4, of which 4 were waited for; matrix products, arithmetic and copies ran while one was open for 0% of the time, Pallas kernels for 4%

profile of v4, /device:TPU:1, one launch (start us, length us, event | category | flops | bytes accessed | tf_op | source)
XLA Modules:
  0.0 142.1 jit_solution(7113131620737829321)
XLA Ops:
  0.0 0.1 pad_add_fusion
  0.1 10.8 %planes.1 = f32[32,2,2,2,8,8,128]{6,5,4,3,2,1,0:T(8,128)} custom-call(f32[2,8,256,256]{3,2,1,0:T(8,128)} %right_ref.1, f32[2,8,256,256]{3,2,1,0:T(8,128)} %right_ref.1, f32[2,8,256,256]{3,2,1,0:T(8,128)} %right_up_ref.1, f32[2,8,256,256]{3,2,1,0:T(8,128)} %right_up_ref.1, bf16[512,256]{1,0:T(8,128)(2,1)} %constant.39.clone.z_ref, ...), custom_call_target="tpu_custom_call" | custom-call | tf_op jit(solution)/shard_map/planes/pallas_call | solution.py:157
  10.9 0.0 copy-start
  10.9 0.0 copy-start.1
  10.9 106.3 %all_to_all.5 = f32[32,2,2,2,8,8,128]{6,5,4,3,2,1,0:T(8,128)S(1)} all-to-all(f32[32,2,2,2,8,8,128]{6,5,4,3,2,1,0:T(8,128)} %planes.1), channel_id=1, replica_groups=mesh['member'=4,'slab'=32] {'slab'}, dimensions={0} | all-to-all | bytes 16777216 | tf_op jit(solution)/shard_map/all_to_all | solution.py:281
  117.2 0.0 copy-done
  117.2 0.0 copy-done.1
  117.2 6.0 %sums.2 = (f32[2,64,8,128]{3,2,1,0:T(8,128)S(1)}, f32[2,64,8,128]{3,2,1,0:T(8,128)S(1)}) custom-call(s32[2]{0:T(128)S(1)} %get-tuple-element.20.place_ref, f32[32,2,2,2,64,128]{5,4,3,2,1,0:T(8,128)S(1)} %bitcast.20, f32[2,2,4,64,2,8,128]{6,5,4,3,2,1,0:T(8,128)S(1)} %bitcast.22, bf16[4,2,64,512]{3,2,1,0:T(8,128)(2,1)S(1)} %copy-done.1), custom_call_target="tpu_custom_call" | custom-call | flops 3221225472 | bytes 33554432 | tf_op jit(solution)/shard_map/sums/pallas_call | solution.py:241
  123.3 2.8 %collective-permute-start = (f32[2,64,8,128]{3,2,1,0:T(8,128)S(1)}, f32[2,64,8,128]{3,2,1,0:T(8,128)S(1)}, u32[]{:S(2)}, u32[]{:S(2)}) collective-permute-start(f32[2,64,8,128]{3,2,1,0:T(8,128)S(1)} %get-tuple-element.22), channel_id=1, source_target_pairs={{0,32},{32,0},{64,96},{96,64},{1,33},{33,1},{65,97},{97,65},{2,34}... | collective-permute-start | bytes 1572872 | tf_op jit(solution)/shard_map/ppermute | solution.py:272
  126.0 1.5 %collective-permute-done = f32[2,64,8,128]{3,2,1,0:T(8,128)S(1)} collective-permute-done((f32[2,64,8,128]{3,2,1,0:T(8,128)S(1)}, f32[2,64,8,128]{3,2,1,0:T(8,128)S(1)}, u32[]{:S(2)}, u32[]{:S(2)}) %collective-permute-start) | collective-permute-done | bytes 524320 | tf_op jit(solution)/shard_map/ppermute | solution.py:272
  127.6 0.1 add.15
  127.6 0.0 copy-start.2
  127.7 1.0 collective-permute-start.3
  128.7 6.0 %sums.3 = (f32[2,64,8,128]{3,2,1,0:T(8,128)S(1)}, f32[2,64,8,128]{3,2,1,0:T(8,128)S(1)}) custom-call(s32[2]{0:T(128)S(1)} %get-tuple-element.24.place_ref, f32[32,2,2,2,64,128]{5,4,3,2,1,0:T(8,128)S(1)} %bitcast.21, f32[2,2,4,64,2,8,128]{6,5,4,3,2,1,0:T(8,128)S(1)} %bitcast.23, bf16[4,2,64,512]{3,2,1,0:T(8,128)(2,1)S(1)} %copy-done.1), custom_call_target="tpu_custom_call" | custom-call | flops 3221225472 | bytes 33554432 | tf_op jit(solution)/shard_map/sums/pallas_call | solution.py:241
  134.7 0.7 collective-permute-start.1
  135.5 0.1 collective-permute-start.2
  135.6 1.1 collective-permute-done.1
  136.6 0.4 collective-permute-done.2
  137.0 4.1 %collective-permute-done.3 = f32[2,64,8,128]{3,2,1,0:T(8,128)S(1)} collective-permute-done((f32[2,64,8,128]{3,2,1,0:T(8,128)S(1)}, f32[2,64,8,128]{3,2,1,0:T(8,128)S(1)}, u32[]{:S(2)}, u32[]{:S(2)}) %collective-permute-start.3) | collective-permute-done | bytes 524320 | tf_op jit(solution)/shard_map/ppermute | solution.py:272
  141.0 0.0 copy-done.2
  141.1 1.0 copy_bitcast_fusion
  (1 shorter events, 0.0 us)
Async XLA Ops:
  10.9 106.3 %copy-start = (f32[2,2,256,8,256]{4,3,2,1,0:T(8,128)S(1)}, f32[2,2,256,8,256]{4,3,2,1,0:T(8,128)}, u32[]{:S(2)}) copy-start(f32[2,2,256,8,256]{4,3,2,1,0:T(8,128)} %param.10) | copy-start | bytes 25165828
  10.9 106.3 %copy-start.1 = (bf16[4,2,64,512]{3,2,1,0:T(8,128)(2,1)S(1)}, bf16[4,2,64,512]{3,2,1,0:T(8,128)(2,1)}, u32[]{:S(2)}) copy-start(bf16[4,2,64,512]{3,2,1,0:T(8,128)(2,1)} %constant.41.clone.x_ref) | copy-start | bytes 1572868
  123.3 4.3 %collective-permute-start = (f32[2,64,8,128]{3,2,1,0:T(8,128)S(1)}, f32[2,64,8,128]{3,2,1,0:T(8,128)S(1)}, u32[]{:S(2)}, u32[]{:S(2)}) collective-permute-start(f32[2,64,8,128]{3,2,1,0:T(8,128)S(1)} %get-tuple-element.22), channel_id=1, source_target_pairs={{0,32},{32,0},{64,96},{96,64},{1,33},{33,1},{65,97},{97,65},{2,34}... | collective-permute-start | bytes 1572872 | tf_op jit(solution)/shard_map/ppermute | solution.py:272
  127.6 13.4 %copy-start.2 = (f32[64,8,256]{2,1,0:T(8,128)S(1)}, f32[64,8,256]{2,1,0:T(8,128)}, u32[]{:S(2)}) copy-start(f32[64,8,256]{2,1,0:T(8,128)} %param.11) | copy-start | bytes 1572868
  127.7 13.4 %collective-permute-start.3 = (f32[2,64,8,128]{3,2,1,0:T(8,128)S(1)}, f32[2,64,8,128]{3,2,1,0:T(8,128)S(1)}, u32[]{:S(2)}, u32[]{:S(2)}) collective-permute-start(f32[2,64,8,128]{3,2,1,0:T(8,128)S(1)} %add.15), channel_id=1, source_target_pairs={{0,64},{32,96},{64,0},{96,32},{1,65},{33,97},{65,1},{97,33},{2,66}... | collective-permute-start | bytes 1572872 | tf_op jit(solution)/shard_map/ppermute | solution.py:272
  134.7 1.9 %collective-permute-start.1 = (f32[1,64,8,128]{3,2,1,0:T(8,128)S(1)}, f32[1,64,8,128]{3,2,1,0:T(8,128)S(1)}, u32[]{:S(2)}, u32[]{:S(2)}) collective-permute-start(f32[1,64,8,128]{3,2,1,0:T(8,128)S(1)} %get-tuple-element.27), channel_id=1, source_target_pairs={{0,32},{32,0},{64,96},{96,64},{1,33},{33,1},{65,97},{97,65},{2,34}... | collective-permute-start | bytes 786440 | tf_op jit(solution)/shard_map/ppermute | solution.py:272
  135.5 1.5 %collective-permute-start.2 = (f32[1,64,8,128]{3,2,1,0:T(8,128)S(1)}, f32[1,64,8,128]{3,2,1,0:T(8,128)S(1)}, u32[]{:S(2)}, u32[]{:S(2)}) collective-permute-start(f32[1,64,8,128]{3,2,1,0:T(8,128)S(1)} %get-tuple-element.28), channel_id=1, source_target_pairs={{0,32},{32,0},{64,96},{96,64},{1,33},{33,1},{65,97},{97,65},{2,34}... | collective-permute-start | bytes 786440 | tf_op jit(solution)/shard_map/ppermute | solution.py:272

commit v5 on v4

--- a/solution.py
+++ b/solution.py
@@ -75,7 +75,9 @@
 
 def times(table, values):
     high, low = halve(values)
-    return dot(table[:, :256], high) + dot(table[:, 256:], high) + dot(table[:, :256], low)
+    rows = table.shape[0]
+    both = dot(jnp.concatenate((table[:, :256], table[:, 256:]), axis=0), high)
+    return both[:rows] + both[rows:] + dot(table[:, :256], low)
 
 
 def planes_kernel(left_ref, right_ref, left_up_ref, right_up_ref, z_ref, y_ref, out_ref):
@@ -190,22 +192,17 @@
             block = received_ref[first : first + 16, side, part, m, pl.ds(k, 8, stride=8), :]
             return block.reshape(half, 128)
 
-        def stacked(sign):
+        def stacked(first):
             return jnp.concatenate(
                 [
-                    jnp.concatenate(
-                        [
-                            samples(0, part, 2 * pair + k) + sign * samples(16, part, 2 * pair + k)
-                            for k in range(2)
-                        ],
-                        axis=1,
-                    )
+                    jnp.concatenate([samples(first, part, 2 * pair + k) for k in range(2)], axis=1)
                     for part in range(2)
                 ],
                 axis=0,
             )
 
-        return [times(tables[parity], stacked(1 - 2 * parity)) for parity in range(2)]
+        low, high = stacked(0), stacked(16)
+        return times(tables[0], low + high), times(tables[1], low - high)
 
     def weighted(side, m, pair, pieces, earlier):
         values = {}

time: 142 us -> 142 us (level)
  no operation moved by 1% of the time
where the time goes in v5:
time: 142 us
  blocking collectives  106 us (75%)
  Pallas kernels  22.2 us (16%)
  waiting for transfers between devices  7.34 us (5%)
  starting transfers between devices  4.63 us (3%)
    all_to_all x1, blocking collectives, body(): lax.all_to_all(sent, 'slab', split_axis=0, concat_axis=0, tiled=True)  106 us
    pallas_call x2, Pallas kernels, sums(): pl.pallas_call(functools.partial(sums_kernel, sides), out_shape=(out, out...  11.4 us
    pallas_call x1, Pallas kernels, planes(): pl.pallas_call(planes_kernel, out_shape=jax.ShapeDtypeStruct((devices_sla...  10.8 us
    ppermute x4, waiting for transfers between devices, swap(): lax.ppermute(values, 'member', [(i, i ^ flip) for i in range(devices_memb...  7.34 us
    ppermute x4, starting transfers between devices, swap(): lax.ppermute(values, 'member', [(i, i ^ flip) for i in range(devices_memb...  4.63 us
  transfers between devices with their start and end apart: 4, of which 4 were waited for; matrix products, arithmetic and copies ran while one was open for 0% of the time, Pallas kernels for 4%

profile of v5, /device:TPU:1, one launch (start us, length us, event | category | flops | bytes accessed | tf_op | source)
XLA Modules:
  0.0 141.7 jit_solution(7234321641045859887)
XLA Ops:
  0.0 0.1 pad_add_fusion
  0.1 10.8 %planes.1 = f32[32,2,2,2,8,8,128]{6,5,4,3,2,1,0:T(8,128)} custom-call(f32[2,8,256,256]{3,2,1,0:T(8,128)} %right_ref.1, f32[2,8,256,256]{3,2,1,0:T(8,128)} %right_ref.1, f32[2,8,256,256]{3,2,1,0:T(8,128)} %right_up_ref.1, f32[2,8,256,256]{3,2,1,0:T(8,128)} %right_up_ref.1, bf16[512,256]{1,0:T(8,128)(2,1)} %constant.39.clone.z_ref, ...), custom_call_target="tpu_custom_call" | custom-call | tf_op jit(solution)/shard_map/planes/pallas_call | solution.py:159
  10.9 0.0 copy-start
  10.9 0.0 copy-start.1
  10.9 106.3 %all_to_all.5 = f32[32,2,2,2,8,8,128]{6,5,4,3,2,1,0:T(8,128)S(1)} all-to-all(f32[32,2,2,2,8,8,128]{6,5,4,3,2,1,0:T(8,128)} %planes.1), channel_id=1, replica_groups=mesh['member'=4,'slab'=32] {'slab'}, dimensions={0} | all-to-all | bytes 16777216 | tf_op jit(solution)/shard_map/all_to_all | solution.py:278
  117.2 0.0 copy-done
  117.2 0.0 copy-done.1
  117.2 5.7 %sums.2 = (f32[2,64,8,128]{3,2,1,0:T(8,128)S(1)}, f32[2,64,8,128]{3,2,1,0:T(8,128)S(1)}) custom-call(s32[2]{0:T(128)S(1)} %get-tuple-element.20.place_ref, f32[32,2,2,2,64,128]{5,4,3,2,1,0:T(8,128)S(1)} %bitcast.20, f32[2,2,4,64,2,8,128]{6,5,4,3,2,1,0:T(8,128)S(1)} %bitcast.22, bf16[4,2,64,512]{3,2,1,0:T(8,128)(2,1)S(1)} %copy-done.1), custom_call_target="tpu_custom_call" | custom-call | flops 3221225472 | bytes 33554432 | tf_op jit(solution)/shard_map/sums/pallas_call | solution.py:238
  122.9 2.8 %collective-permute-start = (f32[2,64,8,128]{3,2,1,0:T(8,128)S(1)}, f32[2,64,8,128]{3,2,1,0:T(8,128)S(1)}, u32[]{:S(2)}, u32[]{:S(2)}) collective-permute-start(f32[2,64,8,128]{3,2,1,0:T(8,128)S(1)} %get-tuple-element.22), channel_id=1, source_target_pairs={{0,32},{32,0},{64,96},{96,64},{1,33},{33,1},{65,97},{97,65},{2,34}... | collective-permute-start | bytes 1572872 | tf_op jit(solution)/shard_map/ppermute | solution.py:269
  125.7 1.5 %collective-permute-done = f32[2,64,8,128]{3,2,1,0:T(8,128)S(1)} collective-permute-done((f32[2,64,8,128]{3,2,1,0:T(8,128)S(1)}, f32[2,64,8,128]{3,2,1,0:T(8,128)S(1)}, u32[]{:S(2)}, u32[]{:S(2)}) %collective-permute-start) | collective-permute-done | bytes 524320 | tf_op jit(solution)/shard_map/ppermute | solution.py:269
  127.2 0.1 add.15
  127.3 0.0 copy-start.2
  127.3 1.0 collective-permute-start.3
  128.3 5.7 %sums.3 = (f32[2,64,8,128]{3,2,1,0:T(8,128)S(1)}, f32[2,64,8,128]{3,2,1,0:T(8,128)S(1)}) custom-call(s32[2]{0:T(128)S(1)} %get-tuple-element.24.place_ref, f32[32,2,2,2,64,128]{5,4,3,2,1,0:T(8,128)S(1)} %bitcast.21, f32[2,2,4,64,2,8,128]{6,5,4,3,2,1,0:T(8,128)S(1)} %bitcast.23, bf16[4,2,64,512]{3,2,1,0:T(8,128)(2,1)S(1)} %copy-done.1), custom_call_target="tpu_custom_call" | custom-call | flops 3221225472 | bytes 33554432 | tf_op jit(solution)/shard_map/sums/pallas_call | solution.py:238
  134.1 0.7 collective-permute-start.1
  134.8 0.1 collective-permute-start.2
  134.9 1.1 collective-permute-done.1
  136.0 0.4 collective-permute-done.2
  136.3 4.4 %collective-permute-done.3 = f32[2,64,8,128]{3,2,1,0:T(8,128)S(1)} collective-permute-done((f32[2,64,8,128]{3,2,1,0:T(8,128)S(1)}, f32[2,64,8,128]{3,2,1,0:T(8,128)S(1)}, u32[]{:S(2)}, u32[]{:S(2)}) %collective-permute-start.3) | collective-permute-done | bytes 524320 | tf_op jit(solution)/shard_map/ppermute | solution.py:269
  140.7 0.0 copy-done.2
  140.7 1.0 copy_bitcast_fusion
  (1 shorter events, 0.0 us)
Async XLA Ops:
  10.9 106.3 %copy-start = (f32[2,2,256,8,256]{4,3,2,1,0:T(8,128)S(1)}, f32[2,2,256,8,256]{4,3,2,1,0:T(8,128)}, u32[]{:S(2)}) copy-start(f32[2,2,256,8,256]{4,3,2,1,0:T(8,128)} %param.10) | copy-start | bytes 25165828
  10.9 106.3 %copy-start.1 = (bf16[4,2,64,512]{3,2,1,0:T(8,128)(2,1)S(1)}, bf16[4,2,64,512]{3,2,1,0:T(8,128)(2,1)}, u32[]{:S(2)}) copy-start(bf16[4,2,64,512]{3,2,1,0:T(8,128)(2,1)} %constant.41.clone.x_ref) | copy-start | bytes 1572868
  122.9 4.3 %collective-permute-start = (f32[2,64,8,128]{3,2,1,0:T(8,128)S(1)}, f32[2,64,8,128]{3,2,1,0:T(8,128)S(1)}, u32[]{:S(2)}, u32[]{:S(2)}) collective-permute-start(f32[2,64,8,128]{3,2,1,0:T(8,128)S(1)} %get-tuple-element.22), channel_id=1, source_target_pairs={{0,32},{32,0},{64,96},{96,64},{1,33},{33,1},{65,97},{97,65},{2,34}... | collective-permute-start | bytes 1572872 | tf_op jit(solution)/shard_map/ppermute | solution.py:269
  127.3 13.4 %copy-start.2 = (f32[64,8,256]{2,1,0:T(8,128)S(1)}, f32[64,8,256]{2,1,0:T(8,128)}, u32[]{:S(2)}) copy-start(f32[64,8,256]{2,1,0:T(8,128)} %param.11) | copy-start | bytes 1572868
  127.3 13.4 %collective-permute-start.3 = (f32[2,64,8,128]{3,2,1,0:T(8,128)S(1)}, f32[2,64,8,128]{3,2,1,0:T(8,128)S(1)}, u32[]{:S(2)}, u32[]{:S(2)}) collective-permute-start(f32[2,64,8,128]{3,2,1,0:T(8,128)S(1)} %add.15), channel_id=1, source_target_pairs={{0,64},{32,96},{64,0},{96,32},{1,65},{33,97},{65,1},{97,33},{2,66}... | collective-permute-start | bytes 1572872 | tf_op jit(solution)/shard_map/ppermute | solution.py:269
  134.1 1.9 %collective-permute-start.1 = (f32[1,64,8,128]{3,2,1,0:T(8,128)S(1)}, f32[1,64,8,128]{3,2,1,0:T(8,128)S(1)}, u32[]{:S(2)}, u32[]{:S(2)}) collective-permute-start(f32[1,64,8,128]{3,2,1,0:T(8,128)S(1)} %get-tuple-element.27), channel_id=1, source_target_pairs={{0,32},{32,0},{64,96},{96,64},{1,33},{33,1},{65,97},{97,65},{2,34}... | collective-permute-start | bytes 786440 | tf_op jit(solution)/shard_map/ppermute | solution.py:269
  134.8 1.5 %collective-permute-start.2 = (f32[1,64,8,128]{3,2,1,0:T(8,128)S(1)}, f32[1,64,8,128]{3,2,1,0:T(8,128)S(1)}, u32[]{:S(2)}, u32[]{:S(2)}) collective-permute-start(f32[1,64,8,128]{3,2,1,0:T(8,128)S(1)} %get-tuple-element.28), channel_id=1, source_target_pairs={{0,32},{32,0},{64,96},{96,64},{1,33},{33,1},{65,97},{97,65},{2,34}... | collective-permute-start | bytes 786440 | tf_op jit(solution)/shard_map/ppermute | solution.py:269
